TPU v7x, 512 devices: a whole 4x8x8 slice. The times are simulated.
512 devices in a mesh: visit: 64 (over y_hi, z, core), strip: 8 (over x, y_lo).
Axes of the slice: x: 4, y: 8 (y_hi: 4, y_lo: 2; y = y_hi * 2 + y_lo), z: 8, core: 2. Of those that a mesh axis runs over, the one named last changes fastest.
Arguments:
- images: float32 [64, 512, 256], P('visit', 'strip')
- variances: float32 [64, 512, 256], P('visit', 'strip'), may hold values from 0.25 to 4
- masks: int32 [64, 512, 256], P('visit', 'strip'), may hold values from 0 to 4095, as said below
- visit_ids: int32 [64], P('visit'), may hold values from 0 to 63, each once
- kernels: float32 [64, 3, 2, 21], replicated, may hold values from 0.01 to 0.09
- amplitudes: float32 [64, 3], replicated, may hold values from 0.5 to 2
- shapes: float32 [64, 3, 5], replicated, may hold values from -0.18 to 0.18
Outputs:
- coadd: float32 [512, 256], P(('strip', 'visit'))
- depth: float32 [512, 256], P(('strip', 'visit'))
Inputs may be any that keep to these rules, and one draw needn't show every extreme that they name: `masks`: A visit pixel is used where bits 0, 1 and 2 of its mask are all clear; bits 3 to 11 are other mask planes. Every pixel is used in at least 3 visits.
All inputs are finite; a program needn't handle non-finite values.
Results may differ from a plain program's by a relative error of at most 0.0003.
Values sent between devices are 32-bit elements; how exact they have to be, the bound alone decides.
No kernel may reach another device: no remote copies, remote signals or barrier semaphores. Data moves between devices by JAX's collectives and lax.ppermute only.
A program may use at most 64 MiB of HBM per device.

v0:
```python
import jax
import jax.numpy as jnp
from jax import lax
from jax.sharding import PartitionSpec as P

pair_first = (0, 1, 2, 0, 0, 1)
pair_second = (0, 1, 2, 1, 2, 2)
pair_count = (1.0, 1.0, 1.0, 2.0, 2.0, 2.0)


def extended_2(block, sides, width):
    for axis, dim in sides:
        count = lax.axis_size(axis)
        forward = [(i, i + 1) for i in range(count - 1)]
        backward = [(target, source) for source, target in forward]
        low = lax.ppermute(
            lax.slice_in_dim(block, block.shape[dim] - width, None, axis=dim), axis, forward
        )
        high = lax.ppermute(lax.slice_in_dim(block, 0, width, axis=dim), axis, backward)
        block = jnp.concatenate([low, block, high], axis=dim)
    return block


def band_from_offsets(taps, offset):
    span = taps.shape[-1]
    result = taps[:, 0, None, None] * (offset == 0).astype(jnp.float32)[None]
    for lag in range(1, span):
        result = result + taps[:, lag, None, None] * (offset == lag).astype(jnp.float32)[None]
    return result


def column_matrices(col_taps, width):
    half = col_taps.shape[-1] // 2
    index = jnp.arange(width, dtype=jnp.int32)
    offset = index[:, None] - index[None, :] + half
    return band_from_offsets(col_taps, offset)


def row_matrices(row_taps, rows):
    span = row_taps.shape[-1]
    extended = rows + span - 1
    offset = (
        jnp.arange(extended, dtype=jnp.int32)[None, :] - jnp.arange(rows, dtype=jnp.int32)[:, None]
    )
    return band_from_offsets(row_taps, offset)


def separable(field, row_taps, col_taps, rows):
    width = field.shape[-1]
    across = jnp.einsum(
        "yx,jxz->jyz",
        field,
        column_matrices(col_taps, width),
        precision=lax.Precision.HIGHEST,
        preferred_element_type=jnp.float32,
    )
    return jnp.einsum(
        "jay,jyz->jaz",
        row_matrices(row_taps, rows),
        across,
        precision=lax.Precision.HIGHEST,
        preferred_element_type=jnp.float32,
    )


def spatial(amplitude, shape, ys, xs):
    terms = 1.0 + shape[:, 0, None, None] * xs + shape[:, 1, None, None] * ys
    terms = terms + shape[:, 2, None, None] * (xs * xs) + shape[:, 3, None, None] * (xs * ys)
    terms = terms + shape[:, 4, None, None] * (ys * ys)
    return amplitude[:, None, None] * terms


def visit_terms(
    image_rows, variance_rows, mask, row_taps, col_taps, amplitude, shape, ys, xs, rows
):
    basis = separable(image_rows, row_taps, col_taps, rows)
    pair_rows = jnp.stack([row_taps[a] * row_taps[b] for a, b in zip(pair_first, pair_second)])
    pair_cols = jnp.stack([col_taps[a] * col_taps[b] for a, b in zip(pair_first, pair_second)])
    paired = separable(variance_rows, pair_rows, pair_cols, rows)
    factor = spatial(amplitude, shape, ys, xs)
    matched = jnp.sum(factor * basis, axis=0)
    cross = jnp.stack(
        [pair_count[p] * factor[pair_first[p]] * factor[pair_second[p]] for p in range(6)]
    )
    matched_var = jnp.sum(cross * paired, axis=0)
    valid = jnp.bitwise_and(mask, 7) == 0
    weight = valid.astype(jnp.float32) / matched_var
    return (matched, weight, valid)


def pick_extreme(values, weights, lowest):
    if lowest:
        where = jnp.argmin(values, axis=0)
    else:
        where = jnp.argmax(values, axis=0)
    chosen = jnp.take_along_axis(values, where[None], axis=0)[0]
    chosen_weight = jnp.take_along_axis(weights, where[None], axis=0)[0]
    return (chosen, chosen_weight)


def shards(images, variances, masks, visit_ids, kernels, amplitudes, shapes):
    slots, rows, width = images.shape
    half = kernels.shape[-1] // 2
    stacked = jnp.stack([images, variances])
    padded = extended_2(stacked, (("strip", 2),), half)
    all_visits = kernels.shape[0]
    onehot = (visit_ids[:, None] == jnp.arange(all_visits, dtype=jnp.int32)[None, :]).astype(
        jnp.float32
    )

    def lookup(table):
        flat = table.reshape(all_visits, -1)
        picked = jnp.dot(onehot, flat, precision=lax.Precision.HIGHEST)
        return picked.reshape((slots,) + table.shape[1:])

    taps = lookup(kernels)
    amplitude = lookup(amplitudes)
    shape = lookup(shapes)
    height = rows * lax.axis_size("strip")
    first_row = lax.axis_index("strip") * rows
    ys = (
        (2 * (first_row + jnp.arange(rows, dtype=jnp.int32)) + 1).astype(jnp.float32) / height - 1.0
    )[:, None]
    xs = ((2 * jnp.arange(width, dtype=jnp.int32) + 1).astype(jnp.float32) / width - 1.0)[None, :]

    def one_slot(inputs):
        image_rows, variance_rows, mask, slot_taps, slot_amplitude, slot_shape = inputs
        return visit_terms(
            image_rows,
            variance_rows,
            mask,
            slot_taps[:, 0],
            slot_taps[:, 1],
            slot_amplitude,
            slot_shape,
            ys,
            xs,
            rows,
        )

    matched, weight, valid = lax.map(
        one_slot, (padded[0], padded[1], masks, taps, amplitude, shape)
    )
    total = jnp.sum(weight * matched, axis=0)
    weights = jnp.sum(weight, axis=0)
    low_value, low_weight = pick_extreme(jnp.where(valid, matched, jnp.inf), weight, True)
    high_value, high_weight = pick_extreme(jnp.where(valid, matched, -jnp.inf), weight, False)
    total, weights = (
        lax.psum_scatter(total, "visit", scatter_dimension=0, tiled=True),
        lax.psum_scatter(weights, "visit", scatter_dimension=0, tiled=True),
    )
    moved = (
        lax.all_to_all(low_value[None], "visit", split_axis=1, concat_axis=0, tiled=True),
        lax.all_to_all(low_weight[None], "visit", split_axis=1, concat_axis=0, tiled=True),
        lax.all_to_all(high_value[None], "visit", split_axis=1, concat_axis=0, tiled=True),
        lax.all_to_all(high_weight[None], "visit", split_axis=1, concat_axis=0, tiled=True),
    )
    low_value, low_weight = pick_extreme(moved[0], moved[1], True)
    high_value, high_weight = pick_extreme(moved[2], moved[3], False)
    coadd = (total - low_weight * low_value - high_weight * high_value) / (
        weights - low_weight - high_weight
    )
    depth = jnp.log(weights + 1.0)
    return (coadd, depth)


def solution(mesh):
    in_specs = (
        P("visit", "strip", None),
        P("visit", "strip", None),
        P("visit", "strip", None),
        P("visit"),
        P(),
        P(),
        P(),
    )
    out_specs = (P(("strip", "visit"), None), P(("strip", "visit"), None))
    return jax.shard_map(shards, mesh=mesh, in_specs=in_specs, out_specs=out_specs, check_vma=False)
```

profile of v0, /device:TPU:7, one launch (start us, length us, event | category | flops | bytes accessed | tf_op | source)
XLA Modules:
  0.0 1167.5 jit_solution(81448529748775)
XLA Ops:
  7.2 1.4 pad_maximum_fusion.2
  8.6 3.5 collective-permute-start.1
  12.1 2.4 collective-permute-start
  14.7 0.8 fusion.197
  15.6 0.8 fusion.195
  16.4 0.8 fusion.193
  17.2 0.8 fusion.191
  19.7 1.1 slice_reduce_fusion.62
  20.8 0.7 slice_reduce_fusion.61
  21.6 1.0 slice_reduce_fusion.83
  22.6 0.6 fusion.424
  23.2 0.6 fusion.422
  23.8 0.6 fusion.420
  24.5 0.6 fusion.418
  25.1 0.6 fusion.416
  25.8 0.6 fusion.414
  26.4 0.6 fusion.412
  27.0 0.6 fusion.410
  27.7 0.6 fusion.408
  28.3 0.6 fusion.406
  29.0 1.0 slice_reduce_fusion.20
  30.0 0.8 slice_reduce_fusion.19
  32.0 0.7 copy-done.53
  32.8 1.1 slice_reduce_fusion.41
  34.1 0.7 slice_reduce_fusion.40
  34.8 1.3 dynamic-slice.1
  36.2 0.9 pad_maximum_fusion
  37.5 3.6 fusion.44
  41.5 1.3 fusion.43
  44.1 199.4 %gather_fusion.1 = f32[16384]{0:T(1024)} fusion(f32[1,64,256]{2,1,0:T(8,128)S(1)} %get-tuple-element.136, s32[16384]{0:T(1024)S(1)} %bitcast.174), kind=kCustom, calls=%fused_computation.2.clone | custom fusion | bytes 327680 | tf_op jit(solution)/shard_map/jit(take_along_axis)/gather | solution.py:96
  243.4 17.4 %all-to-all-start.1 = ((f32[1,64,256]{2,0,1:T(1,128)}), f32[1,64,256]{2,0,1:T(1,128)S(1)}, u32[]{:S(2)}, u32[]{:S(2)}) async-start(f32[1,64,256]{2,0,1:T(1,128)} %bitcast.190), calls=%async_computation.1 | async-start | bytes 131072 | tf_op jit(solution)/shard_map/all_to_all | solution.py:153
  261.2 5.5 fusion
  267.1 1.6 fusion.42
  268.8 0.6 fusion.342
  269.4 199.3 %gather_fusion = f32[16384]{0:T(1024)} fusion(f32[1,64,256]{2,1,0:T(8,128)S(1)} %get-tuple-element.139, s32[16384]{0:T(1024)S(1)} %bitcast.175), kind=kCustom, calls=%fused_computation.clone | custom fusion | bytes 327680 | tf_op jit(solution)/shard_map/jit(take_along_axis)/gather | solution.py:97
  468.7 199.2 %gather_fusion.4 = f32[16384]{0:T(1024)} fusion(f32[1,64,256]{2,1,0:T(8,128)S(1)} %get-tuple-element.142, s32[16384]{0:T(1024)S(1)} %bitcast.176), kind=kCustom, calls=%fused_computation.3.clone | custom fusion | bytes 327680 | tf_op jit(solution)/shard_map/jit(take_along_axis)/gather | solution.py:96
  668.0 12.7 %all-to-all-start.2 = ((f32[1,64,256]{2,0,1:T(1,128)}), f32[1,64,256]{2,0,1:T(1,128)S(1)}, u32[]{:S(2)}, u32[]{:S(2)}) async-start(f32[1,64,256]{2,0,1:T(1,128)} %bitcast.73), calls=%async_computation.2 | async-start | bytes 131072 | tf_op jit(solution)/shard_map/all_to_all | solution.py:155
  680.7 0.6 bitcast_reduce_fusion.1
  681.4 11.4 all-to-all-done.2
  692.8 4.4 all-to-all-start
  697.2 0.6 bitcast_reduce_fusion
  697.9 2.4 gather_fusion.6
  700.3 9.1 all-to-all-done
  709.4 2.4 gather_fusion.5
  711.8 2.4 gather_fusion.2
  714.2 2.4 gather_fusion.3
  716.6 442.1 %all-reduce.5.cloned.1.call-done = (f32[64,256]{1,0:T(8,128)}, f32[64,256]{1,0:T(8,128)}) async-done(((f32[64,256]{1,0:T(8,128)}, f32[64,256]{1,0:T(8,128)}), (f32[64,256]{1,0:T(8,128)}, f32[64,256]{1,0:T(8,128)})) %all-reduce.5.cloned.1.call-update) | async-done | bytes 131088
  1158.7 1.9 add_log_fusion
  (242 shorter events, 4.3 us)
Async XLA Ops:
  7.2 24.2 %copy-start = (f32[64,3]{0,1:T(4,128)S(1)}, f32[64,3]{0,1:T(4,128)}, u32[]{:S(2)}) copy-start(f32[64,3]{0,1:T(4,128)} %param.16) | copy-start | bytes 2308
  8.6 27.6 %collective-permute-start.1 = (f32[2,1,10,256]{3,2,1,0:T(8,128)}, f32[2,1,10,256]{3,2,1,0:T(8,128)}, u32[]{:S(2)}, u32[]{:S(2)}) collective-permute-start(f32[2,1,10,256]{3,2,1,0:T(8,128)} %get-tuple-element.141), channel_id=1, source_target_pairs={{1,0},{2,1},{3,2},{4,3},{5,4},{6,5},{7,6},{9,8},{10,9},{11,10},{12... | collective-permute-start | bytes 61448 | tf_op jit(solution)/shard_map/ppermute | solution.py:19
  12.1 24.1 %collective-permute-start = (f32[2,1,10,256]{3,2,1,0:T(8,128)}, f32[2,1,10,256]{3,2,1,0:T(8,128)}, u32[]{:S(2)}, u32[]{:S(2)}) collective-permute-start(f32[2,1,10,256]{3,2,1,0:T(8,128)} %get-tuple-element.140), channel_id=1, source_target_pairs={{0,1},{1,2},{2,3},{3,4},{4,5},{5,6},{6,7},{8,9},{9,10},{10,11},{11... | collective-permute-start | bytes 61448 | tf_op jit(solution)/shard_map/ppermute | solution.py:16
  18.7 12.1 %copy-start.55 = (f32[64,3,5]{0,1,2:T(4,128)S(1)}, f32[64,3,5]{0,1,2:T(4,128)}, u32[]{:S(2)}) copy-start(f32[64,3,5]{0,1,2:T(4,128)} %param.17) | copy-start | bytes 11524
  32.0 4.1 copy-start.2
  44.1 216.8 %copy-start.76 = (f32[6]{0:T(128)S(1)}, f32[6]{0:T(128)}, u32[]{:S(2)}) copy-start(f32[6]{0:T(128)} %get-tuple-element.71) | copy-start | bytes 76
  44.1 216.8 %copy-start.77 = (f32[6]{0:T(128)S(1)}, f32[6]{0:T(128)}, u32[]{:S(2)}) copy-start(f32[6]{0:T(128)} %get-tuple-element.72) | copy-start | bytes 76
  44.1 216.8 %copy-start.78 = (f32[6]{0:T(128)S(1)}, f32[6]{0:T(128)}, u32[]{:S(2)}) copy-start(f32[6]{0:T(128)} %get-tuple-element.73) | copy-start | bytes 76
  243.4 424.6 %all-to-all-start.1 = ((f32[1,64,256]{2,0,1:T(1,128)}), f32[1,64,256]{2,0,1:T(1,128)S(1)}, u32[]{:S(2)}, u32[]{:S(2)}) async-start(f32[1,64,256]{2,0,1:T(1,128)} %bitcast.190), calls=%async_computation.1 | async-start | bytes 131072 | tf_op jit(solution)/shard_map/all_to_all | solution.py:153
  260.9 5.9 copy-start.12
  260.9 5.9 copy-start.14
  260.9 5.9 copy-start.16
  260.9 5.9 copy-start.18
  260.9 5.9 copy-start.20
  260.9 5.9 copy-start.22
  260.9 5.9 copy-start.24
  260.9 5.9 copy-start.26
  260.9 5.9 copy-start.28
  260.9 5.9 copy-start.30
  261.0 5.9 copy-start.32
  261.0 5.9 copy-start.34
  261.0 5.9 copy-start.36
  261.0 5.9 copy-start.38
  261.0 5.9 copy-start.40
  261.0 5.9 copy-start.42
  261.0 5.9 copy-start.44
  261.0 5.9 copy-start.46
  261.0 5.9 copy-start.48
  261.0 5.9 copy-start.50
  261.1 5.9 copy-start.52
  261.1 5.9 copy-start.54
  261.1 5.9 copy-start.79
  261.1 5.9 copy-start.80
  261.1 5.9 copy-start.81
  261.1 5.9 copy-start.82
  261.1 5.9 copy-start.83
  261.1 5.9 copy-start.84
  261.1 5.9 copy-start.85
  261.1 5.9 copy-start.86
  261.2 5.9 copy-start.87
  261.2 5.9 copy-start.88
  261.2 5.9 copy-start.89
  261.2 5.9 copy-start.90
  261.2 5.9 copy-start.91
  269.4 199.3 %copy-start.1 = (f32[1,64,256]{2,1,0:T(8,128)}, f32[1,64,256]{2,1,0:T(8,128)S(1)}, u32[]{:S(2)}) copy-start(f32[1,64,256]{2,1,0:T(8,128)S(1)} %get-tuple-element.139) | copy-start | bytes 196612
  468.7 689.9 %all-reduce.5.cloned.1.call-start = ((), (), s32[]{:S(2)}) async-start(), calls=%async_computation.3 | async-start | bytes 262144
  668.0 24.8 %all-to-all-start.2 = ((f32[1,64,256]{2,0,1:T(1,128)}), f32[1,64,256]{2,0,1:T(1,128)S(1)}, u32[]{:S(2)}, u32[]{:S(2)}) async-start(f32[1,64,256]{2,0,1:T(1,128)} %bitcast.73), calls=%async_computation.2 | async-start | bytes 131072 | tf_op jit(solution)/shard_map/all_to_all | solution.py:155
  692.8 16.6 %all-to-all-start = ((f32[1,64,256]{2,0,1:T(1,128)}), f32[1,64,256]{2,0,1:T(1,128)S(1)}, u32[]{:S(2)}, u32[]{:S(2)}) async-start(f32[1,64,256]{2,0,1:T(1,128)} %bitcast.72), calls=%async_computation | async-start | bytes 131072 | tf_op jit(solution)/shard_map/all_to_all | solution.py:154
  (50 other events, 173.1 us)
Sparse Core Ops, SparseCore 0:
  668.1 490.5 all-reduce.4
where the time goes:
time: 1170 us
  local copies, waits for them, and re-layouts  617 us (53%)
  waiting for transfers between devices  463 us (40%)
  starting transfers between devices  40.4 us (3%)
  other arithmetic  18 us (2%)
  between operations  16.4 us (1%)
  matrix products  12.6 us (1%)
    unnamed x2, waiting for transfers between devices  442 us
    gather x5, local copies, waits for them, and re-layouts, pick_extreme(): chosen = jnp.take_along_axis(values, where[None], axis=0)[0]  403 us
    gather x3, local copies, waits for them, and re-layouts, pick_extreme(): chosen_weight = jnp.take_along_axis(weights, where[None], axis=0)[0]  204 us
  transfers between devices with their start and end apart: 6, of which 3 were waited for; matrix products, arithmetic and copies ran while one was open for 37% of the time, Pallas kernels for 0%

commit v1 on v0

v1 whole, which is shorter than its diff:
```python
import jax
import jax.numpy as jnp
from jax import lax
from jax.experimental import pallas as pl
from jax.experimental.pallas import tpu as pltpu
from jax.sharding import PartitionSpec as P

pair_first = (0, 1, 2, 0, 0, 1)
pair_second = (0, 1, 2, 1, 2, 2)
pair_count = (1.0, 1.0, 1.0, 2.0, 2.0, 2.0)

LANES = 128
EDGE = 16
VMEM_LIMIT = 32 * 1024 * 1024


def shifted_halves(left, right, shift):
    if shift == 0:
        return left, right
    lane = lax.broadcasted_iota(jnp.int32, left.shape, 1)
    turned_left = pltpu.roll(left, (-shift) % LANES, 1)
    turned_right = pltpu.roll(right, (-shift) % LANES, 1)
    zero = jnp.zeros_like(left)
    if shift > 0:
        inside = lane < LANES - shift
        return jnp.where(inside, turned_left, turned_right), jnp.where(inside, turned_right, zero)
    inside = lane >= -shift
    return jnp.where(inside, turned_left, zero), jnp.where(inside, turned_right, turned_left)


def match_kernel(
    ids, images, variances, masks, low, high, kernels, amplitudes, shapes, out, fields, across
):
    rows = images.shape[1]
    span = kernels.shape[-1]
    half = span // 2
    strip_row = lax.axis_index("strip") * rows
    height = rows * lax.axis_size("strip")
    width = images.shape[2]

    for index, own in enumerate((images, variances)):
        fields[index, 0:EDGE] = low[index]
        fields[index, EDGE : EDGE + rows] = own[0]
        fields[index, EDGE + rows :] = high[index]

    def row_tap(j, a):
        return kernels[0, j, 0, a]

    def col_tap(j, a):
        return kernels[0, j, 1, a]

    def taps_of(get, maps, a):
        if maps == 3:
            return [get(j, a) for j in range(3)]
        single = [get(j, a) for j in range(3)]
        return [single[p] * single[q] for p, q in zip(pair_first, pair_second)]

    chunk = 16

    def columns(step, carry):
        start = pl.multiple_of(step * chunk, chunk)
        for field, maps, base in ((0, 3, 0), (1, 6, 3)):
            left = fields[field, pl.ds(start, chunk), 0:LANES]
            right = fields[field, pl.ds(start, chunk), LANES:]
            sums = None
            for a in range(span):
                moved = shifted_halves(left, right, a - half)
                taps = taps_of(col_tap, maps, a)
                terms = [[tap * m for m in moved] for tap in taps]
                if sums is None:
                    sums = terms
                else:
                    sums = [[s + t for s, t in zip(ss, tt)] for ss, tt in zip(sums, terms)]
            for j in range(maps):
                for side in range(2):
                    across[base + j, side, pl.ds(start, chunk), :] = sums[j][side]
        return carry

    lax.fori_loop(0, (rows + 2 * EDGE) // chunk, columns, 0)

    block = 16

    def finish(step, carry):
        start = pl.multiple_of(step * block, block)
        row = lax.broadcasted_iota(jnp.int32, (block, LANES), 0) + (start + strip_row)
        y = (2 * row + 1).astype(jnp.float32) / height - 1.0
        for side in range(2):
            col = lax.broadcasted_iota(jnp.int32, (block, LANES), 1) + side * LANES
            x = (2 * col + 1).astype(jnp.float32) / width - 1.0
            xx, xy, yy = x * x, x * y, y * y
            factor = []
            for j in range(3):
                s = [shapes[0, j, t] for t in range(5)]
                terms = 1.0 + s[0] * x + s[1] * y
                terms = terms + s[2] * xx + s[3] * xy
                terms = terms + s[4] * yy
                factor.append(amplitudes[0, 0, j] * terms)
            results = []
            for maps, base in ((3, 0), (6, 3)):
                sums = None
                for a in range(span):
                    taps = taps_of(row_tap, maps, a)
                    terms = [
                        taps[j] * across[base + j, side, pl.ds(start + EDGE - half + a, block), :]
                        for j in range(maps)
                    ]
                    sums = terms if sums is None else [s + t for s, t in zip(sums, terms)]
                results.append(sums)
            basis, paired = results
            matched = factor[0] * basis[0]
            for j in range(1, 3):
                matched = matched + factor[j] * basis[j]
            spread = None
            for p in range(6):
                cross = factor[pair_first[p]] * factor[pair_second[p]]
                if pair_count[p] != 1.0:
                    cross = (pair_count[p] * factor[pair_first[p]]) * factor[pair_second[p]]
                term = cross * paired[p]
                spread = term if spread is None else spread + term
            mask = masks[0, pl.ds(start, block), side * LANES : (side + 1) * LANES]
            valid = jnp.bitwise_and(mask, 7) == 0
            weight = jnp.where(valid, 1.0 / spread, 0.0)
            out[pl.ds(4 * start + side, block, stride=4), :] = matched
            out[pl.ds(4 * start + 2 + side, block, stride=4), :] = weight
        return carry

    lax.fori_loop(0, rows // block, finish, 0)


def owner_kernel(moved, coadd, depth):
    visits = moved.shape[0] // 4
    for side in range(2):
        matched = moved[pl.ds(side, visits, stride=4), :]
        weight = moved[pl.ds(2 + side, visits, stride=4), :]
        valid = weight > 0.0
        visit = lax.broadcasted_iota(jnp.int32, matched.shape, 0)

        def extreme(values, value):
            first = jnp.min(jnp.where(values == value, visit, visits), axis=0, keepdims=True)
            return jnp.sum(jnp.where(visit == first, weight, 0.0), axis=0, keepdims=True)

        low_values = jnp.where(valid, matched, jnp.inf)
        high_values = jnp.where(valid, matched, -jnp.inf)
        low_value = jnp.min(low_values, axis=0, keepdims=True)
        high_value = jnp.max(high_values, axis=0, keepdims=True)
        low_weight = extreme(low_values, low_value)
        high_weight = extreme(high_values, high_value)
        total = jnp.sum(weight * matched, axis=0, keepdims=True)
        weights = jnp.sum(weight, axis=0, keepdims=True)
        lanes = slice(side * LANES, (side + 1) * LANES)
        coadd[:, lanes] = (total - low_weight * low_value - high_weight * high_value) / (
            weights - low_weight - high_weight
        )
        depth[:, lanes] = jnp.log(weights + 1.0)


def matched_and_weight(
    images, variances, masks, visit_ids, kernels, amplitudes, shapes, low, high
):
    rows, width = images.shape[1:]
    full = rows + 2 * EDGE

    def whole(shape):
        return pl.BlockSpec(shape, lambda i, ids: (0,) * len(shape))

    def chosen(shape):
        return pl.BlockSpec(
            shape,
            lambda i, ids: (ids[0],) + (0,) * (len(shape) - 1),
            memory_space=pltpu.SMEM,
        )

    return pl.pallas_call(
        match_kernel,
        grid_spec=pltpu.PrefetchScalarGridSpec(
            num_scalar_prefetch=1,
            grid=(1,),
            in_specs=[
                whole((1, rows, width)),
                whole((1, rows, width)),
                whole((1, rows, width)),
                whole((2, EDGE, width)),
                whole((2, EDGE, width)),
                chosen((1,) + kernels.shape[1:]),
                chosen((1, 1) + amplitudes.shape[1:]),
                chosen((1,) + shapes.shape[1:]),
            ],
            out_specs=whole((4 * rows, LANES)),
            scratch_shapes=[
                pltpu.VMEM((2, full, width), jnp.float32),
                pltpu.VMEM((9, 2, full, LANES), jnp.float32),
            ],
        ),
        out_shape=jax.ShapeDtypeStruct((4 * rows, LANES), jnp.float32),
        compiler_params=pltpu.CompilerParams(vmem_limit_bytes=VMEM_LIMIT),
    )(visit_ids, images, variances, masks, low, high, kernels, amplitudes[:, None], shapes)


def shards(images, variances, masks, visit_ids, kernels, amplitudes, shapes):
    rows, width = images.shape[1:]
    strips = lax.axis_size("strip")
    visits = lax.axis_size("visit")
    bottom = jnp.concatenate([images[:, rows - EDGE :], variances[:, rows - EDGE :]])
    top = jnp.concatenate([images[:, :EDGE], variances[:, :EDGE]])
    low = lax.ppermute(bottom, "strip", [(i, i + 1) for i in range(strips - 1)])
    high = lax.ppermute(top, "strip", [(i + 1, i) for i in range(strips - 1)])
    sent = matched_and_weight(
        images, variances, masks, visit_ids, kernels, amplitudes, shapes, low, high
    )
    moved = lax.all_to_all(
        sent.reshape(rows, 4, LANES), "visit", split_axis=0, concat_axis=0, tiled=True
    )
    vmem = pl.BlockSpec(memory_space=pltpu.VMEM)
    coadd, depth = pl.pallas_call(
        owner_kernel,
        in_specs=[vmem],
        out_specs=[vmem, vmem],
        out_shape=[jax.ShapeDtypeStruct((1, width), jnp.float32)] * 2,
        compiler_params=pltpu.CompilerParams(vmem_limit_bytes=VMEM_LIMIT),
    )(moved.reshape(visits * 4, LANES))
    return coadd, depth


def solution(mesh):
    in_specs = (
        P("visit", "strip", None),
        P("visit", "strip", None),
        P("visit", "strip", None),
        P("visit"),
        P(),
        P(),
        P(),
    )
    out_specs = (P(("strip", "visit"), None), P(("strip", "visit"), None))
    return jax.shard_map(shards, mesh=mesh, in_specs=in_specs, out_specs=out_specs, check_vma=False)
```

time: 1170 us -> 46.3 us (0.04)
  the two profiles are of different devices: /device:TPU:7 before, /device:TPU:3 now
where the time goes in v1:
time: 46.3 us; the launch traced here: 45.9 us
  blocking collectives  30.3 us (65%)
  starting transfers between devices  6.18 us (13%)
  Pallas kernels  4.88 us (11%)
  local copies, waits for them, and re-layouts  3.18 us (7%)
  between operations  1.37 us (3%)
    all_to_all x1, blocking collectives, shards(): lax.all_to_all(sent.reshape(rows, 4, LANES), 'visit', split_axis=0, conca...  30.3 us
    pallas_call x1, Pallas kernels, matched_and_weight(): pl.pallas_call(match_kernel, grid_spec=pltpu.PrefetchScalarGridSpec(num_s...  4.23 us
    ppermute x1, starting transfers between devices, shards(): low = lax.ppermute(bottom, 'strip', [(i, i + 1) for i in range(strips - 1)])  3.2 us
    ppermute x1, starting transfers between devices, shards(): high = lax.ppermute(top, 'strip', [(i + 1, i) for i in range(strips - 1)])  2.98 us
    unnamed x15, local copies, waits for them, and re-layouts  2.4 us
  transfers between devices with their start and end apart: 2, of which 0 were waited for; matrix products, arithmetic and copies ran while one was open for 1% of the time, Pallas kernels for 0%

profile of v1, /device:TPU:3, one launch (start us, length us, event | category | flops | bytes accessed | tf_op | source)
XLA Modules:
  0.0 45.9 jit_solution(9932763101471952253)
XLA Ops:
  0.6 0.8 %fusion = (f32[1,16,256]{2,1,0:T(8,128)S(1)}, f32[1,16,256]{2,1,0:T(8,128)S(1)}, f32[1,16,256]{2,1,0:T(8,128)S(1)}, f32[1,16,256]{2,1,0:T(8,128)S(1)}) fusion(f32[1,64,256]{2,1,0:T(8,128)} %images.1, f32[1,64,256]{2,1,0:T(8,128)} %variances.1), kind=kLoop, calls=%fused_computation.2 | loop fusion | bytes 131072 | tf_op jit(solution)/shard_map/slice | solution.py:204
  1.4 3.2 %collective-permute-start = (f32[2,16,256]{2,1,0:T(8,128)S(1)}, f32[2,16,256]{2,1,0:T(8,128)S(1)}, u32[]{:S(2)}, u32[]{:S(2)}) collective-permute-start(f32[2,16,256]{2,1,0:T(8,128)S(1)} %pad_maximum_fusion), channel_id=1, source_target_pairs={{0,1},{1,2},{2,3},{3,4},{4,5},{5,6},{6,7},{8,9},{9,10},{10,11},{11... | collective-permute-start | bytes 98312 | tf_op jit(solution)/shard_map/ppermute | solution.py:205
  4.6 0.0 copy-start.5
  4.7 3.0 %collective-permute-start.1 = (f32[2,16,256]{2,1,0:T(8,128)S(1)}, f32[2,16,256]{2,1,0:T(8,128)S(1)}, u32[]{:S(2)}, u32[]{:S(2)}) collective-permute-start(f32[2,16,256]{2,1,0:T(8,128)S(1)} %pad_maximum_fusion.1), channel_id=1, source_target_pairs={{1,0},{2,1},{3,2},{4,3},{5,4},{6,5},{7,6},{9,8},{10,9},{11,10},{12... | collective-permute-start | bytes 98312 | tf_op jit(solution)/shard_map/ppermute | solution.py:206
  8.3 0.0 copy-done.5
  8.3 0.0 copy-start.4
  8.3 0.1 copy.9
  8.4 0.6 %copy-done.4 = f32[64,3,5]{0,1,2:T(4,128)S(1)} copy-done((f32[64,3,5]{0,1,2:T(4,128)S(1)}, f32[64,3,5]{0,1,2:T(4,128)}, u32[]{:S(2)}) %copy-start.4) | copy-done | bytes 3864
  9.0 0.0 copy-start.3
  9.0 0.1 copy.11.shapes
  9.1 0.7 %copy-done.3 = f32[64,3,2,21]{0,2,3,1:T(2,128)S(1)} copy-done((f32[64,3,2,21]{0,2,3,1:T(2,128)S(1)}, f32[64,3,2,21]{0,2,3,1:T(2,128)}, u32[]{:S(2)}) %copy-start.3) | copy-done | bytes 32280
  9.8 0.0 copy-start
  9.8 0.0 copy-start.1
  9.8 0.0 copy-start.2
  9.8 0.2 copy.10.kernels
  10.0 0.0 collective-permute-done.low
  10.0 0.0 collective-permute-done.1.high
  10.0 0.6 %copy-done = f32[1,64,256]{2,1,0:T(8,128)S(1)} copy-done((f32[1,64,256]{2,1,0:T(8,128)S(1)}, f32[1,64,256]{2,1,0:T(8,128)}, u32[]{:S(2)}) %copy-start) | copy-done | bytes 65560
  10.7 0.0 copy-done.1
  10.7 0.0 copy-done.2
  10.7 4.2 %shard_map.86 = f32[256,128]{1,0:T(8,128)S(1)} custom-call(s32[1]{0:T(128)S(6)} %copy.12.ids, f32[1,64,256]{2,1,0:T(8,128)S(1)} %copy-done, f32[1,64,256]{2,1,0:T(8,128)S(1)} %copy-done.1, s32[1,64,256]{2,1,0:T(8,128)S(1)} %copy-done.2, f32[2,16,256]{2,1,0:T(8,128)S(1)} %collective-permute-done.low, f32[2,16,256]{2,1,0:T(8,128)S(1)} %collective-permute-done.1.high, ...), custom_call_target="tpu_custom_call" | custom-call | tf_op jit(solution)/shard_map/pallas_call | solution.py:173
  15.0 30.3 %all_to_all.5 = f32[64,4,128]{2,1,0:T(4,128)S(1)} all-to-all(f32[64,4,128]{2,1,0:T(4,128)S(1)} %bitcast.3), channel_id=1, replica_groups=mesh['visit'=64,'strip'=8] {'visit'}, dimensions={0} | all-to-all | bytes 262144 | tf_op jit(solution)/shard_map/all_to_all | solution.py:210
  45.2 0.7 %shard_map.87 = (f32[1,256]{1,0:T(1,128)}, f32[1,256]{1,0:T(1,128)}) custom-call(f32[256,128]{1,0:T(8,128)S(1)} %bitcast.4), custom_call_target="tpu_custom_call" | custom-call | tf_op jit(solution)/shard_map/pallas_call | solution.py:214
  (2 shorter events, 0.0 us)
Async XLA Ops:
  1.4 8.6 %collective-permute-start = (f32[2,16,256]{2,1,0:T(8,128)S(1)}, f32[2,16,256]{2,1,0:T(8,128)S(1)}, u32[]{:S(2)}, u32[]{:S(2)}) collective-permute-start(f32[2,16,256]{2,1,0:T(8,128)S(1)} %pad_maximum_fusion), channel_id=1, source_target_pairs={{0,1},{1,2},{2,3},{3,4},{4,5},{5,6},{6,7},{8,9},{9,10},{10,11},{11... | collective-permute-start | bytes 98312 | tf_op jit(solution)/shard_map/ppermute | solution.py:205
  4.6 3.7 %copy-start.5 = (f32[64,3]{0,1:T(4,128)S(1)}, f32[64,3]{0,1:T(4,128)}, u32[]{:S(2)}) copy-start(f32[64,3]{0,1:T(4,128)} %param.12) | copy-start | bytes 2308
  4.7 5.4 %collective-permute-start.1 = (f32[2,16,256]{2,1,0:T(8,128)S(1)}, f32[2,16,256]{2,1,0:T(8,128)S(1)}, u32[]{:S(2)}, u32[]{:S(2)}) collective-permute-start(f32[2,16,256]{2,1,0:T(8,128)S(1)} %pad_maximum_fusion.1), channel_id=1, source_target_pairs={{1,0},{2,1},{3,2},{4,3},{5,4},{6,5},{7,6},{9,8},{10,9},{11,10},{12... | collective-permute-start | bytes 98312 | tf_op jit(solution)/shard_map/ppermute | solution.py:206
  8.3 0.7 %copy-start.4 = (f32[64,3,5]{0,1,2:T(4,128)S(1)}, f32[64,3,5]{0,1,2:T(4,128)}, u32[]{:S(2)}) copy-start(f32[64,3,5]{0,1,2:T(4,128)} %param.13) | copy-start | bytes 11524
  9.0 0.8 %copy-start.3 = (f32[64,3,2,21]{0,2,3,1:T(2,128)S(1)}, f32[64,3,2,21]{0,2,3,1:T(2,128)}, u32[]{:S(2)}) copy-start(f32[64,3,2,21]{0,2,3,1:T(2,128)} %param.11) | copy-start | bytes 96772
  9.8 0.8 %copy-start = (f32[1,64,256]{2,1,0:T(8,128)S(1)}, f32[1,64,256]{2,1,0:T(8,128)}, u32[]{:S(2)}) copy-start(f32[1,64,256]{2,1,0:T(8,128)} %images.1) | copy-start | bytes 196612
  9.8 0.9 %copy-start.1 = (f32[1,64,256]{2,1,0:T(8,128)S(1)}, f32[1,64,256]{2,1,0:T(8,128)}, u32[]{:S(2)}) copy-start(f32[1,64,256]{2,1,0:T(8,128)} %variances.1) | copy-start | bytes 196612
  9.8 0.9 %copy-start.2 = (s32[1,64,256]{2,1,0:T(8,128)S(1)}, s32[1,64,256]{2,1,0:T(8,128)}, u32[]{:S(2)}) copy-start(s32[1,64,256]{2,1,0:T(8,128)} %masks.1) | copy-start | bytes 196612

commit v2 on v1

v2 whole, which is shorter than its diff:
```python
import jax
import jax.numpy as jnp
from jax import lax
from jax.experimental import pallas as pl
from jax.experimental.pallas import tpu as pltpu
from jax.sharding import PartitionSpec as P

pair_first = (0, 1, 2, 0, 0, 1)
pair_second = (0, 1, 2, 1, 2, 2)
pair_count = (1.0, 1.0, 1.0, 2.0, 2.0, 2.0)

LANES = 128
EDGE = 16
VMEM_LIMIT = 32 * 1024 * 1024


def shifted_halves(left, right, shift):
    if shift == 0:
        return left, right
    lane = lax.broadcasted_iota(jnp.int32, left.shape, 1)
    turned_left = pltpu.roll(left, (-shift) % LANES, 1)
    turned_right = pltpu.roll(right, (-shift) % LANES, 1)
    zero = jnp.zeros_like(left)
    if shift > 0:
        inside = lane < LANES - shift
        return jnp.where(inside, turned_left, turned_right), jnp.where(inside, turned_right, zero)
    inside = lane >= -shift
    return jnp.where(inside, turned_left, zero), jnp.where(inside, turned_right, turned_left)


def add_terms(sums, terms):
    return terms if sums is None else [s + t for s, t in zip(sums, terms)]


def columns(images, variances, taps, source, across, target, count):
    span = taps.shape[1]
    for field, maps, base in ((images, 3, 0), (variances, 6, 3)):
        left = field[pl.ds(source, count), 0:LANES]
        right = field[pl.ds(source, count), LANES:]
        sums = None
        for a in range(span):
            moved = shifted_halves(left, right, a - span // 2)
            terms = []
            for j in range(base, base + maps):
                tap = taps[j, a, pl.ds(1, 1), :]
                terms += [tap * m for m in moved]
            sums = add_terms(sums, terms)
        for j in range(maps):
            for side in range(2):
                across[base + j, side, pl.ds(target, count), :] = sums[2 * j + side]


def matched_rows(across, taps, coefs, first, count, offsets, row, height, width, store):
    span = taps.shape[1]
    results = []
    for maps, base in ((3, 0), (6, 3)):
        sums = None
        for a, offset in offsets:
            terms = []
            for j in range(base, base + maps):
                tap = taps[j, a, pl.ds(0, 1), :]
                terms += [tap * across[j, side, pl.ds(first + offset, count), :] for side in range(2)]
            sums = add_terms(sums, terms)
        results += sums
    y = (2 * row + 1).astype(jnp.float32) / height - 1.0
    for side in range(2):
        basis, paired = results[side:6:2], results[6 + side :: 2]
        col = lax.broadcasted_iota(jnp.int32, (count, LANES), 1) + side * LANES
        x = (2 * col + 1).astype(jnp.float32) / width - 1.0
        xx, xy, yy = x * x, x * y, y * y
        factor = []
        for j in range(3):
            s = [coefs[pl.ds(3 * t + j, 1), :] for t in range(6)]
            terms = 1.0 + s[0] * x + s[1] * y
            terms = terms + s[2] * xx + s[3] * xy
            terms = terms + s[4] * yy
            factor.append(s[5] * terms)
        matched = factor[0] * basis[0]
        for j in range(1, 3):
            matched = matched + factor[j] * basis[j]
        spread = None
        for p in range(6):
            cross = factor[pair_first[p]]
            if pair_count[p] != 1.0:
                cross = pair_count[p] * cross
            term = cross * factor[pair_second[p]] * paired[p]
            spread = term if spread is None else spread + term
        store(side, matched, spread)


def of_visit(visit, table):
    here = lax.broadcasted_iota(jnp.int32, table.shape, table.ndim - 1) == visit
    value = jnp.sum(jnp.where(here, table, 0.0), axis=-1, keepdims=True)
    return jnp.broadcast_to(value, table.shape[:-1] + (LANES,))


def edge_kernel(
    ids, kernels, amplitudes, shapes, images, variances,
    below, above, edges, taps, coefs,
    padded, image_ends, variance_ends, tap_table, amplitude_table, shape_table, sems,
):
    rows, width = images.shape[1:]
    span = kernels.shape[1]
    half = span // 2
    copies = [
        (kernels, tap_table),
        (amplitudes, amplitude_table),
        (shapes, shape_table),
        (images.at[0, pl.ds(0, EDGE)], image_ends.at[pl.ds(0, EDGE)]),
        (images.at[0, pl.ds(rows - EDGE, EDGE)], image_ends.at[pl.ds(EDGE, EDGE)]),
        (variances.at[0, pl.ds(0, EDGE)], variance_ends.at[pl.ds(0, EDGE)]),
        (variances.at[0, pl.ds(rows - EDGE, EDGE)], variance_ends.at[pl.ds(EDGE, EDGE)]),
    ]
    copies = [pltpu.make_async_copy(a, b, sems.at[i]) for i, (a, b) in enumerate(copies)]
    for copy in copies:
        copy.start()
    strip_row = lax.axis_index("strip") * rows
    height = rows * lax.axis_size("strip")
    zero = jnp.zeros((9, 2, EDGE, LANES), jnp.float32)
    padded[:, :, 0:EDGE] = zero
    padded[:, :, 2 * EDGE : 3 * EDGE] = zero
    for copy in copies:
        copy.wait()

    visit = ids[0]
    taps[0:3] = of_visit(visit, tap_table[...])
    for p, (i, j) in enumerate(zip(pair_first, pair_second)):
        taps[3 + p] = taps[i] * taps[j]
    for t in range(5):
        coefs[3 * t : 3 * t + 3] = of_visit(visit, shape_table[t])
    coefs[15:18] = of_visit(visit, amplitude_table[...])

    for which, out in ((0, below), (1, above)):
        columns(image_ends, variance_ends, taps, which * EDGE, padded, EDGE, EDGE)
        edges[which] = padded[:, :, EDGE : 2 * EDGE]
        if which == 0:
            offsets = [(a, a - half) for a in range(half + 1, span)]
            first, start = 0, -EDGE
        else:
            offsets = [(a, a - half + EDGE) for a in range(0, half)]
            first, start = EDGE, rows
        row = lax.broadcasted_iota(jnp.int32, (EDGE, LANES), 0) + (strip_row + start)

        def store(side, matched, spread):
            out[side] = matched
            out[2 + side] = spread

        matched_rows(padded, taps, coefs, first, EDGE, offsets, row, height, width, store)


def strip_kernel(images, variances, edges, taps, coefs, out, across):
    rows, width = images.shape[1:]
    span = taps.shape[1]
    half = span // 2
    strip_row = lax.axis_index("strip") * rows
    height = rows * lax.axis_size("strip")
    zero = jnp.zeros((9, 2, EDGE, LANES), jnp.float32)
    across[:, :, 0:EDGE] = zero
    across[:, :, EDGE : 2 * EDGE] = edges[0]
    across[:, :, rows : rows + EDGE] = edges[1]
    across[:, :, rows + EDGE :] = zero

    chunk = 16

    def inner(step, carry):
        start = pl.multiple_of(step * chunk, chunk)
        columns(
            images.at[0], variances.at[0], taps, start + EDGE, across, start + 2 * EDGE, chunk
        )
        return carry

    lax.fori_loop(0, (rows - 2 * EDGE) // chunk, inner, 0)

    block = 16

    def finish(step, carry):
        start = pl.multiple_of(step * block, block)
        row = lax.broadcasted_iota(jnp.int32, (block, LANES), 0) + (start + strip_row)
        offsets = [(a, EDGE - half + a) for a in range(span)]

        def store(side, matched, spread):
            out[side, pl.ds(start, block), :] = matched
            out[2 + side, pl.ds(start, block), :] = spread

        matched_rows(across, taps, coefs, start, block, offsets, row, height, width, store)
        return carry

    lax.fori_loop(0, rows // block, finish, 0)


def weight_kernel(own, masks, low, high, out):
    rows = own.shape[1]
    for side in range(2):
        mask = masks[0, :, side * LANES : (side + 1) * LANES]
        for start, extra in ((0, low), (EDGE, None), (rows - EDGE, high)):
            count = EDGE if extra is not None else rows - 2 * EDGE
            matched = own[side, start : start + count, :]
            spread = own[2 + side, start : start + count, :]
            if extra is not None:
                matched = matched + extra[side]
                spread = spread + extra[2 + side]
            valid = jnp.bitwise_and(mask[start : start + count], 7) == 0
            out[pl.ds(4 * start + side, count, stride=4), :] = matched
            out[pl.ds(4 * start + 2 + side, count, stride=4), :] = jnp.where(valid, 1.0 / spread, 0.0)


def owner_kernel(moved, coadd, depth):
    visits = moved.shape[0] // 4
    for side in range(2):
        matched = moved[pl.ds(side, visits, stride=4), :]
        weight = moved[pl.ds(2 + side, visits, stride=4), :]
        valid = weight > 0.0
        visit = lax.broadcasted_iota(jnp.int32, matched.shape, 0)

        def extreme(values, value):
            first = jnp.min(jnp.where(values == value, visit, visits), axis=0, keepdims=True)
            return jnp.sum(jnp.where(visit == first, weight, 0.0), axis=0, keepdims=True)

        low_values = jnp.where(valid, matched, jnp.inf)
        high_values = jnp.where(valid, matched, -jnp.inf)
        low_value = jnp.min(low_values, axis=0, keepdims=True)
        high_value = jnp.max(high_values, axis=0, keepdims=True)
        low_weight = extreme(low_values, low_value)
        high_weight = extreme(high_values, high_value)
        total = jnp.sum(weight * matched, axis=0, keepdims=True)
        weights = jnp.sum(weight, axis=0, keepdims=True)
        lanes = slice(side * LANES, (side + 1) * LANES)
        coadd[:, lanes] = (total - low_weight * low_value - high_weight * high_value) / (
            weights - low_weight - high_weight
        )
        depth[:, lanes] = jnp.log(weights + 1.0)


VMEM = pl.BlockSpec(memory_space=pltpu.VMEM)
HBM = pl.BlockSpec(memory_space=pltpu.HBM)
SMEM = pl.BlockSpec(memory_space=pltpu.SMEM)
PARAMS = pltpu.CompilerParams(vmem_limit_bytes=VMEM_LIMIT)


def f32(*shape):
    return jax.ShapeDtypeStruct(shape, jnp.float32)


def cost(flops):
    return pl.CostEstimate(flops=flops, bytes_accessed=1 << 20, transcendentals=0)


def edge_parts(ids, kernels, amplitudes, shapes, images, variances):
    width = images.shape[2]
    return pl.pallas_call(
        edge_kernel,
        in_specs=[SMEM] + [HBM] * 5,
        out_specs=[VMEM] * 5,
        out_shape=[
            f32(4, EDGE, LANES),
            f32(4, EDGE, LANES),
            f32(2, 9, 2, EDGE, LANES),
            f32(9, *kernels.shape[1:3], LANES),
            f32(18, LANES),
        ],
        scratch_shapes=[
            pltpu.VMEM((9, 2, 3 * EDGE, LANES), jnp.float32),
            pltpu.VMEM((2 * EDGE, width), jnp.float32),
            pltpu.VMEM((2 * EDGE, width), jnp.float32),
            pltpu.VMEM(kernels.shape, jnp.float32),
            pltpu.VMEM(amplitudes.shape, jnp.float32),
            pltpu.VMEM(shapes.shape, jnp.float32),
            pltpu.SemaphoreType.DMA((7,)),
        ],
        compiler_params=PARAMS,
    )(
        ids,
        *(
            pltpu.with_memory_space_constraint(x, pltpu.HBM)
            for x in (kernels, amplitudes, shapes, images, variances)
        ),
    )


def strip_parts(images, variances, edges, taps, coefs):
    rows = images.shape[1]
    return pl.pallas_call(
        strip_kernel,
        in_specs=[VMEM] * 5,
        out_specs=VMEM,
        out_shape=f32(4, rows, LANES),
        scratch_shapes=[pltpu.VMEM((9, 2, rows + 2 * EDGE, LANES), jnp.float32)],
        compiler_params=PARAMS,
        cost_estimate=cost(20_000_000),
    )(images, variances, edges, taps, coefs)


def weighted(own, masks, low, high):
    rows = own.shape[1]
    return pl.pallas_call(
        weight_kernel,
        in_specs=[VMEM] * 4,
        out_specs=VMEM,
        out_shape=f32(4 * rows, LANES),
        compiler_params=PARAMS,
    )(own, masks, low, high)


def owned(moved, width):
    return pl.pallas_call(
        owner_kernel,
        in_specs=[VMEM],
        out_specs=[VMEM, VMEM],
        out_shape=[f32(1, width)] * 2,
        compiler_params=PARAMS,
    )(moved)


def before_exchange(images, variances, masks, visit_ids, kernels, amplitudes, shapes):
    strips = lax.axis_size("strip")
    below, above, edges, taps, coefs = edge_parts(
        visit_ids,
        jnp.transpose(kernels, (1, 3, 2, 0)),
        jnp.transpose(amplitudes, (1, 0)),
        jnp.transpose(shapes, (2, 1, 0)),
        images,
        variances,
    )
    low = lax.ppermute(above, "strip", [(i, i + 1) for i in range(strips - 1)])
    high = lax.ppermute(below, "strip", [(i + 1, i) for i in range(strips - 1)])
    own = strip_parts(images, variances, edges, taps, coefs)
    return weighted(own, masks, low, high)


def shards(images, variances, masks, visit_ids, kernels, amplitudes, shapes):
    rows, width = images.shape[1:]
    visits = lax.axis_size("visit")
    sent = before_exchange(images, variances, masks, visit_ids, kernels, amplitudes, shapes)
    moved = lax.all_to_all(
        sent.reshape(rows, 4, LANES), "visit", split_axis=0, concat_axis=0, tiled=True
    )
    coadd, depth = owned(moved.reshape(visits * 4, LANES), width)
    return coadd, depth


def solution(mesh):
    in_specs = (
        P("visit", "strip", None),
        P("visit", "strip", None),
        P("visit", "strip", None),
        P("visit"),
        P(),
        P(),
        P(),
    )
    out_specs = (P(("strip", "visit"), None), P(("strip", "visit"), None))
    return jax.shard_map(shards, mesh=mesh, in_specs=in_specs, out_specs=out_specs, check_vma=False)
```

time: 46.3 us -> 43.2 us (0.933)
  the two profiles are of different devices: /device:TPU:3 before, /device:TPU:11 now
where the time goes in v2:
time: 43.2 us; the launch traced here: 42.9 us
  blocking collectives  30.5 us (71%)
  starting transfers between devices  5.28 us (12%)
  Pallas kernels  4.84 us (11%)
  between operations  1.36 us (3%)
  waiting for transfers between devices  0.95 us (2%)
    all_to_all x1, blocking collectives, shards(): lax.all_to_all(sent.reshape(rows, 4, LANES), 'visit', split_axis=0, conca...  30.5 us
    ppermute x1, starting transfers between devices, before_exchange(): low = lax.ppermute(above, 'strip', [(i, i + 1) for i in range(strips - 1)])  3.01 us
    pallas_call x1, Pallas kernels, strip_parts(): pl.pallas_call(strip_kernel, in_specs=[VMEM] * 5, out_specs=VMEM, out_sha...  2.28 us
    ppermute x1, starting transfers between devices, before_exchange(): high = lax.ppermute(below, 'strip', [(i + 1, i) for i in range(strips - 1)])  2.28 us
    pallas_call x1, Pallas kernels, edge_parts(): pl.pallas_call(edge_kernel, in_specs=[SMEM] + [HBM] * 5, out_specs=[VMEM]...  1.89 us
    ppermute x1, waiting for transfers between devices, before_exchange(): high = lax.ppermute(below, 'strip', [(i + 1, i) for i in range(strips - 1)])  0.94 us
  transfers between devices with their start and end apart: 2, of which 1 were waited for; matrix products, arithmetic and copies ran while one was open for 0% of the time, Pallas kernels for 5%

profile of v2, /device:TPU:11, one launch (start us, length us, event | category | flops | bytes accessed | tf_op | source)
XLA Modules:
  0.0 42.9 jit_solution(18151078397830491373)
XLA Ops:
  1.3 0.0 copy-start
  1.3 0.0 copy-start.1
  1.3 1.9 %shard_map.86 = (f32[4,16,128]{2,1,0:T(8,128)S(1)}, f32[4,16,128]{2,1,0:T(8,128)S(1)}, f32[2,9,2,16,128]{4,3,2,1,0:T(8,128)S(1)}, f32[9,21,2,128]{3,2,1,0:T(2,128)S(1)}, f32[18,128]{1,0:T(8,128)S(1)}) custom-call(s32[1]{0:T(128)S(6)} %copy.9.ids, f32[3,21,2,64]{3,2,1,0:T(2,128)} %bitcast.7, f32[3,64]{1,0:T(4,128)} %bitcast.9, f32[5,3,64]{2,1,0:T(4,128)} %bitcast.8, ...), custom_call_target="tpu_custom_call" | custom-call | tf_op jit(solution)/shard_map/pallas_call | solution.py:250
  3.2 3.0 %collective-permute-start = (f32[4,16,128]{2,1,0:T(8,128)S(1)}, f32[4,16,128]{2,1,0:T(8,128)S(1)}, u32[]{:S(2)}, u32[]{:S(2)}) collective-permute-start(f32[4,16,128]{2,1,0:T(8,128)S(1)} %get-tuple-element.10), channel_id=1, source_target_pairs={{0,1},{1,2},{2,3},{3,4},{4,5},{5,6},{6,7},{8,9},{9,10},{10,11},{11... | collective-permute-start | bytes 98312 | tf_op jit(solution)/shard_map/ppermute | solution.py:324
  6.2 2.3 %collective-permute-start.1 = (f32[4,16,128]{2,1,0:T(8,128)S(1)}, f32[4,16,128]{2,1,0:T(8,128)S(1)}, u32[]{:S(2)}, u32[]{:S(2)}) collective-permute-start(f32[4,16,128]{2,1,0:T(8,128)S(1)} %get-tuple-element.11), channel_id=1, source_target_pairs={{1,0},{2,1},{3,2},{4,3},{5,4},{6,5},{7,6},{9,8},{10,9},{11,10},{12... | collective-permute-start | bytes 98312 | tf_op jit(solution)/shard_map/ppermute | solution.py:325
  8.5 0.0 copy-done
  8.5 0.0 copy-done.1
  8.5 0.0 copy-start.2
  8.5 2.3 %shard_map.87.own = f32[4,64,128]{2,1,0:T(8,128)S(1)} custom-call(f32[1,64,256]{2,1,0:T(8,128)S(1)} %copy-done, f32[1,64,256]{2,1,0:T(8,128)S(1)} %copy-done.1, f32[2,9,2,16,128]{4,3,2,1,0:T(8,128)S(1)} %get-tuple-element.7.edges, f32[9,21,2,128]{3,2,1,0:T(2,128)S(1)} %get-tuple-element.8.taps, f32[18,128]{1,0:T(8,128)S(1)} %get-tuple-element.9.coefs), custom_call_target="tpu_custom_call" | custom-call | flops 20000000 | bytes 1048576 | tf_op jit(solution)/shard_map/pallas_call | solution.py:282
  10.8 0.0 collective-permute-done.low
  10.8 0.9 %collective-permute-done.1.high = f32[4,16,128]{2,1,0:T(8,128)S(1)} collective-permute-done((f32[4,16,128]{2,1,0:T(8,128)S(1)}, f32[4,16,128]{2,1,0:T(8,128)S(1)}, u32[]{:S(2)}, u32[]{:S(2)}) %collective-permute-start.1) | collective-permute-done | bytes 32800 | tf_op jit(solution)/shard_map/ppermute | solution.py:325
  11.8 0.0 copy-done.2
  11.8 30.5 %all_to_all.5 = f32[64,4,128]{2,1,0:T(4,128)S(1)} all-to-all(f32[64,4,128]{2,1,0:T(4,128)S(1)} %bitcast.5), channel_id=1, replica_groups=mesh['visit'=64,'strip'=8] {'visit'}, dimensions={0} | all-to-all | bytes 262144 | tf_op jit(solution)/shard_map/all_to_all | solution.py:334
  42.3 0.7 %shard_map.89 = (f32[1,256]{1,0:T(1,128)}, f32[1,256]{1,0:T(1,128)}) custom-call(f32[256,128]{1,0:T(8,128)S(1)} %bitcast.6), custom_call_target="tpu_custom_call" | custom-call | tf_op jit(solution)/shard_map/pallas_call | solution.py:305
  (1 shorter events, 0.0 us)
Async XLA Ops:
  1.3 7.2 %copy-start = (f32[1,64,256]{2,1,0:T(8,128)S(1)}, f32[1,64,256]{2,1,0:T(8,128)}, u32[]{:S(2)}) copy-start(f32[1,64,256]{2,1,0:T(8,128)} %images.3) | copy-start | bytes 196612
  1.3 7.2 %copy-start.1 = (f32[1,64,256]{2,1,0:T(8,128)S(1)}, f32[1,64,256]{2,1,0:T(8,128)}, u32[]{:S(2)}) copy-start(f32[1,64,256]{2,1,0:T(8,128)} %variances.3) | copy-start | bytes 196612
  3.2 7.6 %collective-permute-start = (f32[4,16,128]{2,1,0:T(8,128)S(1)}, f32[4,16,128]{2,1,0:T(8,128)S(1)}, u32[]{:S(2)}, u32[]{:S(2)}) collective-permute-start(f32[4,16,128]{2,1,0:T(8,128)S(1)} %get-tuple-element.10), channel_id=1, source_target_pairs={{0,1},{1,2},{2,3},{3,4},{4,5},{5,6},{6,7},{8,9},{9,10},{10,11},{11... | collective-permute-start | bytes 98312 | tf_op jit(solution)/shard_map/ppermute | solution.py:324
  6.2 5.6 %collective-permute-start.1 = (f32[4,16,128]{2,1,0:T(8,128)S(1)}, f32[4,16,128]{2,1,0:T(8,128)S(1)}, u32[]{:S(2)}, u32[]{:S(2)}) collective-permute-start(f32[4,16,128]{2,1,0:T(8,128)S(1)} %get-tuple-element.11), channel_id=1, source_target_pairs={{1,0},{2,1},{3,2},{4,3},{5,4},{6,5},{7,6},{9,8},{10,9},{11,10},{12... | collective-permute-start | bytes 98312 | tf_op jit(solution)/shard_map/ppermute | solution.py:325
  8.5 3.3 %copy-start.2 = (s32[1,64,256]{2,1,0:T(8,128)S(1)}, s32[1,64,256]{2,1,0:T(8,128)}, u32[]{:S(2)}) copy-start(s32[1,64,256]{2,1,0:T(8,128)} %masks.1) | copy-start | bytes 196612

commit v3 on v2

v3 whole, which is shorter than its diff:
```python
import functools

import jax
import jax.numpy as jnp
from jax import lax
from jax.experimental import pallas as pl
from jax.experimental.pallas import tpu as pltpu
from jax.sharding import PartitionSpec as P

pair_first = (0, 1, 2, 0, 0, 1)
pair_second = (0, 1, 2, 1, 2, 2)
pair_count = (1.0, 1.0, 1.0, 2.0, 2.0, 2.0)

LANES = 128
EDGE = 16
VMEM_LIMIT = 32 * 1024 * 1024


def shifted_halves(left, right, shift):
    if shift == 0:
        return left, right
    lane = lax.broadcasted_iota(jnp.int32, left.shape, 1)
    turned_left = pltpu.roll(left, (-shift) % LANES, 1)
    turned_right = pltpu.roll(right, (-shift) % LANES, 1)
    zero = jnp.zeros_like(left)
    if shift > 0:
        inside = lane < LANES - shift
        return jnp.where(inside, turned_left, turned_right), jnp.where(inside, turned_right, zero)
    inside = lane >= -shift
    return jnp.where(inside, turned_left, zero), jnp.where(inside, turned_right, turned_left)


def add_terms(sums, terms):
    return terms if sums is None else [s + t for s, t in zip(sums, terms)]


def columns(images, variances, taps, source, across, target, count):
    span = taps.shape[1]
    for field, maps, base in ((images, 3, 0), (variances, 6, 3)):
        left = field[pl.ds(source, count), 0:LANES]
        right = field[pl.ds(source, count), LANES:]
        sums = None
        for a in range(span):
            moved = shifted_halves(left, right, a - span // 2)
            terms = []
            for j in range(base, base + maps):
                tap = taps[j, a, pl.ds(1, 1), :]
                terms += [tap * m for m in moved]
            sums = add_terms(sums, terms)
        for j in range(maps):
            for side in range(2):
                across[base + j, side, pl.ds(target, count), :] = sums[2 * j + side]


def row_sums(across, taps, down, tiles, offsets):
    tile = 8
    uses = {}
    for t in range(tiles):
        for a, offset in offsets:
            uses.setdefault(tile * t + offset, []).append((t, a))

    def one_map(j, carry):
        tap = {a: taps[j, a, pl.ds(0, 1), :] for a, offset in offsets}
        sums = [[None] * tiles for side in range(2)]
        for place in sorted(uses):
            for side in range(2):
                rows = across[j, side, pl.ds(place, tile), :]
                for t, a in uses[place]:
                    term = tap[a] * rows
                    sums[side][t] = term if sums[side][t] is None else sums[side][t] + term
        for side in range(2):
            for t in range(tiles):
                down[j, side, tile * t : tile * (t + 1), :] = sums[side][t]
        return carry

    lax.fori_loop(0, 9, one_map, 0, unroll=3)


def combine(down, start, count, coefs, row, height, width, store):
    y = (2 * row + 1).astype(jnp.float32) / height - 1.0
    for side in range(2):
        sums = [down[j, side, pl.ds(start, count), :] for j in range(9)]
        basis, paired = sums[:3], sums[3:]
        col = lax.broadcasted_iota(jnp.int32, (count, LANES), 1) + side * LANES
        x = (2 * col + 1).astype(jnp.float32) / width - 1.0
        xx, xy, yy = x * x, x * y, y * y
        factor = []
        for j in range(3):
            s = [coefs[pl.ds(3 * t + j, 1), :] for t in range(6)]
            terms = 1.0 + s[0] * x + s[1] * y
            terms = terms + s[2] * xx + s[3] * xy
            terms = terms + s[4] * yy
            factor.append(s[5] * terms)
        matched = factor[0] * basis[0]
        for j in range(1, 3):
            matched = matched + factor[j] * basis[j]
        spread = None
        for p in range(6):
            cross = factor[pair_first[p]]
            if pair_count[p] != 1.0:
                cross = pair_count[p] * cross
            term = cross * factor[pair_second[p]] * paired[p]
            spread = term if spread is None else spread + term
        store(side, matched, spread)


def of_visit(visit, table):
    here = lax.broadcasted_iota(jnp.int32, table.shape, table.ndim - 1) == visit
    value = jnp.sum(jnp.where(here, table, 0.0), axis=-1, keepdims=True)
    return jnp.broadcast_to(value, table.shape[:-1] + (LANES,))


def load_kernel(
    kernels, amplitudes, shapes, images, variances,
    tap_table, amplitude_table, shape_table, bottom, top, sems,
):
    rows = images.shape[1]
    copies = [
        (images.at[0, pl.ds(rows - EDGE, EDGE)], bottom.at[0]),
        (variances.at[0, pl.ds(rows - EDGE, EDGE)], bottom.at[1]),
        (images.at[0, pl.ds(0, EDGE)], top.at[0]),
        (variances.at[0, pl.ds(0, EDGE)], top.at[1]),
        (kernels, tap_table),
        (amplitudes, amplitude_table),
        (shapes, shape_table),
    ]
    copies = [pltpu.make_async_copy(a, b, sems.at[i]) for i, (a, b) in enumerate(copies)]
    for copy in copies:
        copy.start()
    for copy in copies:
        copy.wait()


def strip_kernel(
    ids, tap_table, amplitude_table, shape_table, images, variances, masks,
    out, taps, coefs, across, down,
):
    rows, width = images.shape[1:]
    span = taps.shape[1]
    half = span // 2
    strip_row = lax.axis_index("strip") * rows
    height = rows * lax.axis_size("strip")
    zero = jnp.zeros((9, 2, EDGE, LANES), jnp.float32)
    across[:, :, 0:EDGE] = zero
    across[:, :, rows + EDGE :] = zero

    visit = ids[0]
    taps[0:3] = of_visit(visit, tap_table[...])
    for p, (i, j) in enumerate(zip(pair_first, pair_second)):
        taps[3 + p] = taps[i] * taps[j]
    for t in range(5):
        coefs[3 * t : 3 * t + 3] = of_visit(visit, shape_table[t])
    coefs[15:18] = of_visit(visit, amplitude_table[...])

    chunk = 32

    def inner(step, carry):
        start = pl.multiple_of(step * chunk, chunk)
        columns(images.at[0], variances.at[0], taps, start, across, start + EDGE, chunk)
        return carry

    lax.fori_loop(0, rows // chunk, inner, 0)
    row_sums(across, taps, down, rows // 8, [(a, EDGE - half + a) for a in range(span)])

    block = 32
    for start in range(0, rows, block):
        row = lax.broadcasted_iota(jnp.int32, (block, LANES), 0) + (start + strip_row)

        def store(side, matched, spread):
            mask = masks[0, pl.ds(start, block), side * LANES : (side + 1) * LANES]
            valid = jnp.bitwise_and(mask, 7) == 0
            out[side, pl.ds(start, block), :] = matched
            out[2 + side, pl.ds(start, block), :] = jnp.where(valid, spread, jnp.inf)

        combine(down, start, block, coefs, row, height, width, store)


def halo_part(halo, taps, coefs, padded, down, rows, width, start, offsets, source, store):
    strip_row = lax.axis_index("strip") * rows
    height = rows * lax.axis_size("strip")
    padded[:, :, EDGE - source : 2 * EDGE - source] = jnp.zeros((9, 2, EDGE, LANES), jnp.float32)
    columns(halo.at[0], halo.at[1], taps, 0, padded, source, EDGE)
    row_sums(padded, taps, down, EDGE // 8, offsets)
    row = lax.broadcasted_iota(jnp.int32, (EDGE, LANES), 0) + (strip_row + start)
    combine(down, 0, EDGE, coefs, row, height, width, store)


def low_kernel(rows, low, taps, coefs, out, padded, down):
    half = taps.shape[1] // 2

    def store(side, matched, spread):
        out[side] = matched
        out[2 + side] = spread

    offsets = [(a, EDGE - half + a) for a in range(half)]
    halo_part(low, taps, coefs, padded, down, rows, low.shape[2], 0, offsets, 0, store)


def weight_kernel(own, first, high, taps, coefs, out, padded, down, last):
    rows = own.shape[1]
    span = taps.shape[1]
    half = span // 2

    def store(side, matched, spread):
        last[side] = matched
        last[2 + side] = spread

    offsets = [(a, a - half) for a in range(half + 1, span)]
    halo_part(
        high, taps, coefs, padded, down, rows, high.shape[2], rows - EDGE, offsets, EDGE, store
    )
    for side in range(2):
        for start, extra in ((0, first), (EDGE, None), (rows - EDGE, last)):
            count = EDGE if extra is not None else rows - 2 * EDGE
            matched = own[side, start : start + count, :]
            spread = own[2 + side, start : start + count, :]
            if extra is not None:
                matched = matched + extra[side]
                spread = spread + extra[2 + side]
            out[pl.ds(4 * start + side, count, stride=4), :] = matched
            out[pl.ds(4 * start + 2 + side, count, stride=4), :] = 1.0 / spread


def owner_kernel(moved, coadd, depth):
    visits = moved.shape[0] // 4
    for side in range(2):
        matched = moved[pl.ds(side, visits, stride=4), :]
        weight = moved[pl.ds(2 + side, visits, stride=4), :]
        valid = weight > 0.0
        visit = lax.broadcasted_iota(jnp.int32, matched.shape, 0)

        def extreme(values, value):
            first = jnp.min(jnp.where(values == value, visit, visits), axis=0, keepdims=True)
            return jnp.sum(jnp.where(visit == first, weight, 0.0), axis=0, keepdims=True)

        low_values = jnp.where(valid, matched, jnp.inf)
        high_values = jnp.where(valid, matched, -jnp.inf)
        low_value = jnp.min(low_values, axis=0, keepdims=True)
        high_value = jnp.max(high_values, axis=0, keepdims=True)
        low_weight = extreme(low_values, low_value)
        high_weight = extreme(high_values, high_value)
        total = jnp.sum(weight * matched, axis=0, keepdims=True)
        weights = jnp.sum(weight, axis=0, keepdims=True)
        lanes = slice(side * LANES, (side + 1) * LANES)
        coadd[:, lanes] = (total - low_weight * low_value - high_weight * high_value) / (
            weights - low_weight - high_weight
        )
        depth[:, lanes] = jnp.log(weights + 1.0)


VMEM = pl.BlockSpec(memory_space=pltpu.VMEM)
HBM = pl.BlockSpec(memory_space=pltpu.HBM)
SMEM = pl.BlockSpec(memory_space=pltpu.SMEM)
PARAMS = pltpu.CompilerParams(vmem_limit_bytes=VMEM_LIMIT)


def f32(*shape):
    return jax.ShapeDtypeStruct(shape, jnp.float32)


def cost(flops):
    return pl.CostEstimate(flops=flops, bytes_accessed=1 << 20, transcendentals=0)


def loaded(kernels, amplitudes, shapes, images, variances):
    width = images.shape[2]
    return pl.pallas_call(
        load_kernel,
        in_specs=[HBM] * 5,
        out_specs=[VMEM] * 5,
        out_shape=[
            f32(*kernels.shape),
            f32(*amplitudes.shape),
            f32(*shapes.shape),
            f32(2, EDGE, width),
            f32(2, EDGE, width),
        ],
        scratch_shapes=[pltpu.SemaphoreType.DMA((7,))],
        compiler_params=PARAMS,
    )(
        *(
            pltpu.with_memory_space_constraint(x, pltpu.HBM)
            for x in (kernels, amplitudes, shapes, images, variances)
        )
    )


def strip_parts(ids, kernels, amplitudes, shapes, images, variances, masks):
    rows = images.shape[1]
    return pl.pallas_call(
        strip_kernel,
        in_specs=[SMEM] + [VMEM] * 6,
        out_specs=[VMEM] * 3,
        out_shape=[f32(4, rows, LANES), f32(9, *kernels.shape[1:3], LANES), f32(18, LANES)],
        scratch_shapes=[
            pltpu.VMEM((9, 2, rows + 2 * EDGE, LANES), jnp.float32),
            pltpu.VMEM((9, 2, rows, LANES), jnp.float32),
        ],
        compiler_params=PARAMS,
        cost_estimate=cost(20_000_000),
    )(ids, kernels, amplitudes, shapes, images, variances, masks)


HALO_SCRATCH = [
    pltpu.VMEM((9, 2, 2 * EDGE, LANES), jnp.float32),
    pltpu.VMEM((9, 2, EDGE, LANES), jnp.float32),
]


def low_part(rows, low, taps, coefs):
    return pl.pallas_call(
        functools.partial(low_kernel, rows),
        in_specs=[VMEM] * 3,
        out_specs=VMEM,
        out_shape=f32(4, EDGE, LANES),
        scratch_shapes=HALO_SCRATCH,
        compiler_params=PARAMS,
        cost_estimate=cost(4_000_000),
    )(low, taps, coefs)


def weighted(own, first, high, taps, coefs):
    rows = own.shape[1]
    return pl.pallas_call(
        weight_kernel,
        in_specs=[VMEM] * 5,
        out_specs=VMEM,
        out_shape=f32(4 * rows, LANES),
        scratch_shapes=HALO_SCRATCH + [pltpu.VMEM((4, EDGE, LANES), jnp.float32)],
        compiler_params=PARAMS,
    )(own, first, high, taps, coefs)


def owned(moved, width):
    return pl.pallas_call(
        owner_kernel,
        in_specs=[VMEM],
        out_specs=[VMEM, VMEM],
        out_shape=[f32(1, width)] * 2,
        compiler_params=PARAMS,
    )(moved)


def before_exchange(images, variances, masks, visit_ids, kernels, amplitudes, shapes):
    strips = lax.axis_size("strip")
    rows = images.shape[1]
    *tables, bottom, top = loaded(
        jnp.transpose(kernels, (1, 3, 2, 0)),
        jnp.transpose(amplitudes, (1, 0)),
        jnp.transpose(shapes, (2, 1, 0)),
        images,
        variances,
    )
    low = lax.ppermute(bottom, "strip", [(i, i + 1) for i in range(strips - 1)])
    high = lax.ppermute(top, "strip", [(i + 1, i) for i in range(strips - 1)])
    own, taps, coefs = strip_parts(visit_ids, *tables, images, variances, masks)
    first = low_part(rows, low, taps, coefs)
    return weighted(own, first, high, taps, coefs)


def shards(images, variances, masks, visit_ids, kernels, amplitudes, shapes):
    rows, width = images.shape[1:]
    visits = lax.axis_size("visit")
    sent = before_exchange(images, variances, masks, visit_ids, kernels, amplitudes, shapes)
    moved = lax.all_to_all(
        sent.reshape(rows, 4, LANES), "visit", split_axis=0, concat_axis=0, tiled=True
    )
    coadd, depth = owned(moved.reshape(visits * 4, LANES), width)
    return coadd, depth


def solution(mesh):
    in_specs = (
        P("visit", "strip", None),
        P("visit", "strip", None),
        P("visit", "strip", None),
        P("visit"),
        P(),
        P(),
        P(),
    )
    out_specs = (P(("strip", "visit"), None), P(("strip", "visit"), None))
    return jax.shard_map(shards, mesh=mesh, in_specs=in_specs, out_specs=out_specs, check_vma=False)
```

time: 43.2 us -> 42.6 us (0.986)
  the two profiles are of different devices: /device:TPU:11 before, /device:TPU:7 now
where the time goes in v3:
time: 42.6 us; the launch traced here: 42.2 us
  blocking collectives  29.7 us (70%)
  starting transfers between devices  6.18 us (15%)
  Pallas kernels  4.93 us (12%)
  between operations  1.38 us (3%)
    all_to_all x1, blocking collectives, shards(): lax.all_to_all(sent.reshape(rows, 4, LANES), 'visit', split_axis=0, conca...  29.7 us
    ppermute x1, starting transfers between devices, before_exchange(): low = lax.ppermute(bottom, 'strip', [(i, i + 1) for i in range(strips - 1)])  3.2 us
    ppermute x1, starting transfers between devices, before_exchange(): high = lax.ppermute(top, 'strip', [(i + 1, i) for i in range(strips - 1)])  2.98 us
    pallas_call x1, Pallas kernels, strip_parts(): pl.pallas_call(strip_kernel, in_specs=[SMEM] + [VMEM] * 6, out_specs=[VME...  2.29 us
    pallas_call x1, Pallas kernels, loaded(): pl.pallas_call(load_kernel, in_specs=[HBM] * 5, out_specs=[VMEM] * 5, out...  1.02 us
  transfers between devices with their start and end apart: 2, of which 0 were waited for; matrix products, arithmetic and copies ran while one was open for 0% of the time, Pallas kernels for 7%

profile of v3, /device:TPU:7, one launch (start us, length us, event | category | flops | bytes accessed | tf_op | source)
XLA Modules:
  0.0 42.2 jit_solution(6070464109205439955)
XLA Ops:
  0.6 0.0 copy-start
  0.6 0.0 copy-start.1
  0.7 0.0 copy-start.2
  0.7 1.0 %shard_map.86 = (f32[3,21,2,64]{3,2,1,0:T(2,128)S(1)}, f32[3,64]{1,0:T(4,128)S(1)}, f32[5,3,64]{2,1,0:T(4,128)S(1)}, f32[2,16,256]{2,1,0:T(8,128)S(1)}, f32[2,16,256]{2,1,0:T(8,128)S(1)}) custom-call(f32[3,21,2,64]{3,2,1,0:T(2,128)} %bitcast.7, f32[3,64]{1,0:T(4,128)} %bitcast.9, f32[5,3,64]{2,1,0:T(4,128)} %bitcast.8, f32[1,64,256]{2,1,0:T(8,128)} %images.3, ...), custom_call_target="tpu_custom_call" | custom-call | tf_op jit(solution)/shard_map/pallas_call | solution.py:267
  1.7 3.2 %collective-permute-start = (f32[2,16,256]{2,1,0:T(8,128)S(1)}, f32[2,16,256]{2,1,0:T(8,128)S(1)}, u32[]{:S(2)}, u32[]{:S(2)}) collective-permute-start(f32[2,16,256]{2,1,0:T(8,128)S(1)} %get-tuple-element.14), channel_id=1, source_target_pairs={{0,1},{1,2},{2,3},{3,4},{4,5},{5,6},{6,7},{8,9},{9,10},{10,11},{11... | collective-permute-start | bytes 98312 | tf_op jit(solution)/shard_map/ppermute | solution.py:354
  4.9 3.0 %collective-permute-start.1 = (f32[2,16,256]{2,1,0:T(8,128)S(1)}, f32[2,16,256]{2,1,0:T(8,128)S(1)}, u32[]{:S(2)}, u32[]{:S(2)}) collective-permute-start(f32[2,16,256]{2,1,0:T(8,128)S(1)} %get-tuple-element.17), channel_id=1, source_target_pairs={{1,0},{2,1},{3,2},{4,3},{5,4},{6,5},{7,6},{9,8},{10,9},{11,10},{12... | collective-permute-start | bytes 98312 | tf_op jit(solution)/shard_map/ppermute | solution.py:355
  8.5 0.0 copy-done
  8.5 0.0 copy-done.1
  8.5 0.0 copy-done.2
  8.6 2.3 %shard_map.87 = (f32[4,64,128]{2,1,0:T(8,128)S(1)}, f32[9,21,2,128]{3,2,1,0:T(2,128)S(1)}, f32[18,128]{1,0:T(8,128)S(1)}) custom-call(s32[1]{0:T(128)S(6)} %copy.9.ids, f32[3,21,2,64]{3,2,1,0:T(2,128)S(1)} %get-tuple-element.10.tap_table, f32[3,64]{1,0:T(4,128)S(1)} %get-tuple-element.11.amplitude_table, f32[5,3,64]{2,1,0:T(4,128)S(1)} %get-tuple-element.12.shape_table, ...), custom_call_target="tpu_custom_call" | custom-call | flops 20000000 | bytes 1048576 | tf_op jit(solution)/shard_map/pallas_call | solution.py:290
  10.9 0.0 collective-permute-done.low
  10.9 0.5 %shard_map.88.first = f32[4,16,128]{2,1,0:T(8,128)S(1)} custom-call(f32[2,16,256]{2,1,0:T(8,128)S(1)} %collective-permute-done.low, f32[9,21,2,128]{3,2,1,0:T(2,128)S(1)} %get-tuple-element.15.taps, f32[18,128]{1,0:T(8,128)S(1)} %get-tuple-element.16.coefs), custom_call_target="tpu_custom_call" | custom-call | flops 4000000 | bytes 1048576 | tf_op jit(solution)/shard_map/pallas_call | solution.py:311
  11.4 0.0 collective-permute-done.1.high
  11.4 0.5 %shard_map.89 = f32[256,128]{1,0:T(8,128)S(1)} custom-call(f32[4,64,128]{2,1,0:T(8,128)S(1)} %get-tuple-element.13.own, f32[4,16,128]{2,1,0:T(8,128)S(1)} %shard_map.88.first, f32[2,16,256]{2,1,0:T(8,128)S(1)} %collective-permute-done.1.high, f32[9,21,2,128]{3,2,1,0:T(2,128)S(1)} %get-tuple-element.15.taps, f32[18,128]{1,0:T(8,128)S(1)} %get-tuple-element.16.coefs), custom_call_target="tpu_custom_call" | custom-call | tf_op jit(solution)/shard_map/pallas_call | solution.py:324
  11.9 29.7 %all_to_all.5 = f32[64,4,128]{2,1,0:T(4,128)S(1)} all-to-all(f32[64,4,128]{2,1,0:T(4,128)S(1)} %bitcast.6), channel_id=1, replica_groups=mesh['visit'=64,'strip'=8] {'visit'}, dimensions={0} | all-to-all | bytes 262144 | tf_op jit(solution)/shard_map/all_to_all | solution.py:365
  41.6 0.7 %shard_map.90 = (f32[1,256]{1,0:T(1,128)}, f32[1,256]{1,0:T(1,128)}) custom-call(f32[256,128]{1,0:T(8,128)S(1)} %bitcast.5), custom_call_target="tpu_custom_call" | custom-call | tf_op jit(solution)/shard_map/pallas_call | solution.py:335
Async XLA Ops:
  0.6 7.9 %copy-start = (f32[1,64,256]{2,1,0:T(8,128)S(1)}, f32[1,64,256]{2,1,0:T(8,128)}, u32[]{:S(2)}) copy-start(f32[1,64,256]{2,1,0:T(8,128)} %images.3) | copy-start | bytes 196612
  0.6 7.9 %copy-start.1 = (f32[1,64,256]{2,1,0:T(8,128)S(1)}, f32[1,64,256]{2,1,0:T(8,128)}, u32[]{:S(2)}) copy-start(f32[1,64,256]{2,1,0:T(8,128)} %variances.3) | copy-start | bytes 196612
  0.7 7.9 %copy-start.2 = (s32[1,64,256]{2,1,0:T(8,128)S(1)}, s32[1,64,256]{2,1,0:T(8,128)}, u32[]{:S(2)}) copy-start(s32[1,64,256]{2,1,0:T(8,128)} %masks.1) | copy-start | bytes 196612
  1.7 9.2 %collective-permute-start = (f32[2,16,256]{2,1,0:T(8,128)S(1)}, f32[2,16,256]{2,1,0:T(8,128)S(1)}, u32[]{:S(2)}, u32[]{:S(2)}) collective-permute-start(f32[2,16,256]{2,1,0:T(8,128)S(1)} %get-tuple-element.14), channel_id=1, source_target_pairs={{0,1},{1,2},{2,3},{3,4},{4,5},{5,6},{6,7},{8,9},{9,10},{10,11},{11... | collective-permute-start | bytes 98312 | tf_op jit(solution)/shard_map/ppermute | solution.py:354
  4.9 6.5 %collective-permute-start.1 = (f32[2,16,256]{2,1,0:T(8,128)S(1)}, f32[2,16,256]{2,1,0:T(8,128)S(1)}, u32[]{:S(2)}, u32[]{:S(2)}) collective-permute-start(f32[2,16,256]{2,1,0:T(8,128)S(1)} %get-tuple-element.17), channel_id=1, source_target_pairs={{1,0},{2,1},{3,2},{4,3},{5,4},{6,5},{7,6},{9,8},{10,9},{11,10},{12... | collective-permute-start | bytes 98312 | tf_op jit(solution)/shard_map/ppermute | solution.py:355

commit v4 on v3

--- a/solution.py
+++ b/solution.py
@@ -110,16 +110,22 @@
     return jnp.broadcast_to(value, table.shape[:-1] + (LANES,))
 
 
+def strip_is_even():
+    return lax.rem(lax.axis_index("strip"), 2) == 0
+
+
 def load_kernel(
     kernels, amplitudes, shapes, images, variances,
-    tap_table, amplitude_table, shape_table, bottom, top, sems,
+    tap_table, amplitude_table, shape_table, sent_first, sent_second, sems,
 ):
     rows = images.shape[1]
+    place = pl.multiple_of(jnp.where(strip_is_even(), rows - EDGE, 0), EDGE)
+    other = pl.multiple_of(jnp.where(strip_is_even(), 0, rows - EDGE), EDGE)
     copies = [
-        (images.at[0, pl.ds(rows - EDGE, EDGE)], bottom.at[0]),
-        (variances.at[0, pl.ds(rows - EDGE, EDGE)], bottom.at[1]),
-        (images.at[0, pl.ds(0, EDGE)], top.at[0]),
-        (variances.at[0, pl.ds(0, EDGE)], top.at[1]),
+        (images.at[0, pl.ds(place, EDGE)], sent_first.at[0]),
+        (variances.at[0, pl.ds(place, EDGE)], sent_first.at[1]),
+        (images.at[0, pl.ds(other, EDGE)], sent_second.at[0]),
+        (variances.at[0, pl.ds(other, EDGE)], sent_second.at[1]),
         (kernels, tap_table),
         (amplitudes, amplitude_table),
         (shapes, shape_table),
@@ -175,45 +181,55 @@
         combine(down, start, block, coefs, row, height, width, store)
 
 
-def halo_part(halo, taps, coefs, padded, down, rows, width, start, offsets, source, store):
-    strip_row = lax.axis_index("strip") * rows
+def halo_part(halo, after, taps, coefs, padded, down, rows, store):
+    span = taps.shape[1]
+    half = span // 2
+    zero = jnp.zeros((9, 2, EDGE, LANES), jnp.float32)
+    padded[:, :, 0:EDGE] = zero
+    padded[:, :, 2 * EDGE :] = zero
+    columns(halo.at[0], halo.at[1], taps, 0, padded, EDGE, EDGE)
+
+    @pl.when(after)
+    def _():
+        row_sums(padded, taps, down, EDGE // 8, [(a, a - half) for a in range(half + 1, span)])
+
+    @pl.when(jnp.logical_not(after))
+    def _():
+        row_sums(padded, taps, down, EDGE // 8, [(a, 2 * EDGE - half + a) for a in range(half)])
+
+    first_row = lax.axis_index("strip") * rows + jnp.where(after, rows - EDGE, 0)
+    row = lax.broadcasted_iota(jnp.int32, (EDGE, LANES), 0) + first_row
     height = rows * lax.axis_size("strip")
-    padded[:, :, EDGE - source : 2 * EDGE - source] = jnp.zeros((9, 2, EDGE, LANES), jnp.float32)
-    columns(halo.at[0], halo.at[1], taps, 0, padded, source, EDGE)
-    row_sums(padded, taps, down, EDGE // 8, offsets)
-    row = lax.broadcasted_iota(jnp.int32, (EDGE, LANES), 0) + (strip_row + start)
-    combine(down, 0, EDGE, coefs, row, height, width, store)
-
-
-def low_kernel(rows, low, taps, coefs, out, padded, down):
-    half = taps.shape[1] // 2
-
+    combine(down, 0, EDGE, coefs, row, height, halo.shape[2], store)
+
+
+def first_kernel(rows, halo, taps, coefs, out, padded, down):
     def store(side, matched, spread):
         out[side] = matched
         out[2 + side] = spread
 
-    offsets = [(a, EDGE - half + a) for a in range(half)]
-    halo_part(low, taps, coefs, padded, down, rows, low.shape[2], 0, offsets, 0, store)
-
-
-def weight_kernel(own, first, high, taps, coefs, out, padded, down, last):
+    halo_part(halo, strip_is_even(), taps, coefs, padded, down, rows, store)
+
+
+def weight_kernel(own, first, halo, taps, coefs, out, padded, down, second):
     rows = own.shape[1]
-    span = taps.shape[1]
-    half = span // 2
+    even = strip_is_even()
 
     def store(side, matched, spread):
-        last[side] = matched
-        last[2 + side] = spread
-
-    offsets = [(a, a - half) for a in range(half + 1, span)]
-    halo_part(
-        high, taps, coefs, padded, down, rows, high.shape[2], rows - EDGE, offsets, EDGE, store
-    )
-    for side in range(2):
-        for start, extra in ((0, first), (EDGE, None), (rows - EDGE, last)):
-            count = EDGE if extra is not None else rows - 2 * EDGE
-            matched = own[side, start : start + count, :]
-            spread = own[2 + side, start : start + count, :]
+        second[side] = matched
+        second[2 + side] = spread
+
+    halo_part(halo, jnp.logical_not(even), taps, coefs, padded, down, rows, store)
+    for extra, start in (
+        (first, jnp.where(even, rows - EDGE, 0)),
+        (None, EDGE),
+        (second, jnp.where(even, 0, rows - EDGE)),
+    ):
+        count = EDGE if extra is not None else rows - 2 * EDGE
+        start = pl.multiple_of(start, EDGE) if extra is not None else start
+        for side in range(2):
+            matched = own[side, pl.ds(start, count), :]
+            spread = own[2 + side, pl.ds(start, count), :]
             if extra is not None:
                 matched = matched + extra[side]
                 spread = spread + extra[2 + side]
@@ -302,24 +318,24 @@
 
 
 HALO_SCRATCH = [
-    pltpu.VMEM((9, 2, 2 * EDGE, LANES), jnp.float32),
+    pltpu.VMEM((9, 2, 3 * EDGE, LANES), jnp.float32),
     pltpu.VMEM((9, 2, EDGE, LANES), jnp.float32),
 ]
 
 
-def low_part(rows, low, taps, coefs):
+def first_part(rows, halo, taps, coefs):
     return pl.pallas_call(
-        functools.partial(low_kernel, rows),
+        functools.partial(first_kernel, rows),
         in_specs=[VMEM] * 3,
         out_specs=VMEM,
         out_shape=f32(4, EDGE, LANES),
         scratch_shapes=HALO_SCRATCH,
         compiler_params=PARAMS,
         cost_estimate=cost(4_000_000),
-    )(low, taps, coefs)
-
-
-def weighted(own, first, high, taps, coefs):
+    )(halo, taps, coefs)
+
+
+def weighted(own, first, halo, taps, coefs):
     rows = own.shape[1]
     return pl.pallas_call(
         weight_kernel,
@@ -328,7 +344,7 @@
         out_shape=f32(4 * rows, LANES),
         scratch_shapes=HALO_SCRATCH + [pltpu.VMEM((4, EDGE, LANES), jnp.float32)],
         compiler_params=PARAMS,
-    )(own, first, high, taps, coefs)
+    )(own, first, halo, taps, coefs)
 
 
 def owned(moved, width):
@@ -344,18 +360,23 @@
 def before_exchange(images, variances, masks, visit_ids, kernels, amplitudes, shapes):
     strips = lax.axis_size("strip")
     rows = images.shape[1]
-    *tables, bottom, top = loaded(
+    *tables, sent_first, sent_second = loaded(
         jnp.transpose(kernels, (1, 3, 2, 0)),
         jnp.transpose(amplitudes, (1, 0)),
         jnp.transpose(shapes, (2, 1, 0)),
         images,
         variances,
     )
-    low = lax.ppermute(bottom, "strip", [(i, i + 1) for i in range(strips - 1)])
-    high = lax.ppermute(top, "strip", [(i + 1, i) for i in range(strips - 1)])
+
+    def swap(edge, start):
+        pairs = [(i, i + 1) for i in range(start, strips - 1, 2)]
+        return lax.ppermute(edge, "strip", pairs + [(b, a) for a, b in pairs])
+
+    halo_first = swap(sent_first, 0)
+    halo_second = swap(sent_second, 1)
     own, taps, coefs = strip_parts(visit_ids, *tables, images, variances, masks)
-    first = low_part(rows, low, taps, coefs)
-    return weighted(own, first, high, taps, coefs)
+    first = first_part(rows, halo_first, taps, coefs)
+    return weighted(own, first, halo_second, taps, coefs)
 
 
 def shards(images, variances, masks, visit_ids, kernels, amplitudes, shapes):

time: 42.6 us -> 42.1 us (0.988)
  starting transfers between devices: 6.18 us -> 5.55 us
    ppermute x2, starting transfers between devices: 6.18 us -> 5.55 us  [swap(): return lax.ppermute(edge, 'strip', pairs + [(b, a) for a, b in pairs])]
where the time goes in v4:
time: 42.1 us; the launch traced here: 41.9 us
  blocking collectives  30 us (71%)
  starting transfers between devices  5.55 us (13%)
  Pallas kernels  4.97 us (12%)
  between operations  1.38 us (3%)
    all_to_all x1, blocking collectives, shards(): lax.all_to_all(sent.reshape(rows, 4, LANES), 'visit', split_axis=0, conca...  30 us
    ppermute x2, starting transfers between devices, swap(): return lax.ppermute(edge, 'strip', pairs + [(b, a) for a, b in pairs])  5.55 us
    pallas_call x1, Pallas kernels, strip_parts(): pl.pallas_call(strip_kernel, in_specs=[SMEM] + [VMEM] * 6, out_specs=[VME...  2.29 us
    pallas_call x1, Pallas kernels, loaded(): pl.pallas_call(load_kernel, in_specs=[HBM] * 5, out_specs=[VMEM] * 5, out...  1.03 us
  transfers between devices with their start and end apart: 2, of which 0 were waited for; matrix products, arithmetic and copies ran while one was open for 0% of the time, Pallas kernels for 7%

profile of v4, /device:TPU:7, one launch (start us, length us, event | category | flops | bytes accessed | tf_op | source)
XLA Modules:
  0.0 41.9 jit_solution(1231943995679333150)
XLA Ops:
  0.6 0.0 copy-start
  0.6 0.0 copy-start.1
  0.7 0.0 copy-start.2
  0.7 1.0 %shard_map.86 = (f32[3,21,2,64]{3,2,1,0:T(2,128)S(1)}, f32[3,64]{1,0:T(4,128)S(1)}, f32[5,3,64]{2,1,0:T(4,128)S(1)}, f32[2,16,256]{2,1,0:T(8,128)S(1)}, f32[2,16,256]{2,1,0:T(8,128)S(1)}) custom-call(f32[3,21,2,64]{3,2,1,0:T(2,128)} %bitcast.7, f32[3,64]{1,0:T(4,128)} %bitcast.9, f32[5,3,64]{2,1,0:T(4,128)} %bitcast.8, f32[1,64,256]{2,1,0:T(8,128)} %images.3, ...), custom_call_target="tpu_custom_call" | custom-call | tf_op jit(solution)/shard_map/pallas_call | solution.py:283
  1.7 3.2 %collective-permute-start = (f32[2,16,256]{2,1,0:T(8,128)S(1)}, f32[2,16,256]{2,1,0:T(8,128)S(1)}, u32[]{:S(2)}, u32[]{:S(2)}) collective-permute-start(f32[2,16,256]{2,1,0:T(8,128)S(1)} %get-tuple-element.14), channel_id=1, source_target_pairs={{0,1},{2,3},{4,5},{6,7},{1,0},{3,2},{5,4},{7,6},{8,9},{10,11},{12,... | collective-permute-start | bytes 98312 | tf_op jit(solution)/shard_map/ppermute | solution.py:373
  4.9 2.3 %collective-permute-start.1 = (f32[2,16,256]{2,1,0:T(8,128)S(1)}, f32[2,16,256]{2,1,0:T(8,128)S(1)}, u32[]{:S(2)}, u32[]{:S(2)}) collective-permute-start(f32[2,16,256]{2,1,0:T(8,128)S(1)} %get-tuple-element.17), channel_id=1, source_target_pairs={{1,2},{3,4},{5,6},{2,1},{4,3},{6,5},{9,10},{11,12},{13,14},{10,9},... | collective-permute-start | bytes 98312 | tf_op jit(solution)/shard_map/ppermute | solution.py:373
  7.9 0.0 copy-done
  7.9 0.0 copy-done.1
  7.9 0.0 copy-done.2
  7.9 2.3 %shard_map.87 = (f32[4,64,128]{2,1,0:T(8,128)S(1)}, f32[9,21,2,128]{3,2,1,0:T(2,128)S(1)}, f32[18,128]{1,0:T(8,128)S(1)}) custom-call(s32[1]{0:T(128)S(6)} %copy.9.ids, f32[3,21,2,64]{3,2,1,0:T(2,128)S(1)} %get-tuple-element.10.tap_table, f32[3,64]{1,0:T(4,128)S(1)} %get-tuple-element.11.amplitude_table, f32[5,3,64]{2,1,0:T(4,128)S(1)} %get-tuple-element.12.shape_table, ...), custom_call_target="tpu_custom_call" | custom-call | flops 20000000 | bytes 1048576 | tf_op jit(solution)/shard_map/pallas_call | solution.py:306
  10.2 0.0 collective-permute-done.halo
  10.2 0.5 %shard_map.88.first = f32[4,16,128]{2,1,0:T(8,128)S(1)} custom-call(f32[2,16,256]{2,1,0:T(8,128)S(1)} %collective-permute-done.halo, f32[9,21,2,128]{3,2,1,0:T(2,128)S(1)} %get-tuple-element.15.taps, f32[18,128]{1,0:T(8,128)S(1)} %get-tuple-element.16.coefs), custom_call_target="tpu_custom_call" | custom-call | flops 4000000 | bytes 1048576 | tf_op jit(solution)/shard_map/pallas_call | solution.py:327
  10.8 0.0 collective-permute-done.1.halo
  10.8 0.5 %shard_map.89 = f32[256,128]{1,0:T(8,128)S(1)} custom-call(f32[4,64,128]{2,1,0:T(8,128)S(1)} %get-tuple-element.13.own, f32[4,16,128]{2,1,0:T(8,128)S(1)} %shard_map.88.first, f32[2,16,256]{2,1,0:T(8,128)S(1)} %collective-permute-done.1.halo, f32[9,21,2,128]{3,2,1,0:T(2,128)S(1)} %get-tuple-element.15.taps, f32[18,128]{1,0:T(8,128)S(1)} %get-tuple-element.16.coefs), custom_call_target="tpu_custom_call" | custom-call | tf_op jit(solution)/shard_map/pallas_call | solution.py:340
  11.3 30.0 %all_to_all.5 = f32[64,4,128]{2,1,0:T(4,128)S(1)} all-to-all(f32[64,4,128]{2,1,0:T(4,128)S(1)} %bitcast.6), channel_id=1, replica_groups=mesh['visit'=64,'strip'=8] {'visit'}, dimensions={0} | all-to-all | bytes 262144 | tf_op jit(solution)/shard_map/all_to_all | solution.py:386
  41.2 0.7 %shard_map.90 = (f32[1,256]{1,0:T(1,128)}, f32[1,256]{1,0:T(1,128)}) custom-call(f32[256,128]{1,0:T(8,128)S(1)} %bitcast.5), custom_call_target="tpu_custom_call" | custom-call | tf_op jit(solution)/shard_map/pallas_call | solution.py:351
Async XLA Ops:
  0.6 7.3 %copy-start = (f32[1,64,256]{2,1,0:T(8,128)S(1)}, f32[1,64,256]{2,1,0:T(8,128)}, u32[]{:S(2)}) copy-start(f32[1,64,256]{2,1,0:T(8,128)} %images.3) | copy-start | bytes 196612
  0.6 7.3 %copy-start.1 = (f32[1,64,256]{2,1,0:T(8,128)S(1)}, f32[1,64,256]{2,1,0:T(8,128)}, u32[]{:S(2)}) copy-start(f32[1,64,256]{2,1,0:T(8,128)} %variances.3) | copy-start | bytes 196612
  0.7 7.3 %copy-start.2 = (s32[1,64,256]{2,1,0:T(8,128)S(1)}, s32[1,64,256]{2,1,0:T(8,128)}, u32[]{:S(2)}) copy-start(s32[1,64,256]{2,1,0:T(8,128)} %masks.1) | copy-start | bytes 196612
  1.7 8.5 %collective-permute-start = (f32[2,16,256]{2,1,0:T(8,128)S(1)}, f32[2,16,256]{2,1,0:T(8,128)S(1)}, u32[]{:S(2)}, u32[]{:S(2)}) collective-permute-start(f32[2,16,256]{2,1,0:T(8,128)S(1)} %get-tuple-element.14), channel_id=1, source_target_pairs={{0,1},{2,3},{4,5},{6,7},{1,0},{3,2},{5,4},{7,6},{8,9},{10,11},{12,... | collective-permute-start | bytes 98312 | tf_op jit(solution)/shard_map/ppermute | solution.py:373
  4.9 5.8 %collective-permute-start.1 = (f32[2,16,256]{2,1,0:T(8,128)S(1)}, f32[2,16,256]{2,1,0:T(8,128)S(1)}, u32[]{:S(2)}, u32[]{:S(2)}) collective-permute-start(f32[2,16,256]{2,1,0:T(8,128)S(1)} %get-tuple-element.17), channel_id=1, source_target_pairs={{1,2},{3,4},{5,6},{2,1},{4,3},{6,5},{9,10},{11,12},{13,14},{10,9},... | collective-permute-start | bytes 98312 | tf_op jit(solution)/shard_map/ppermute | solution.py:373

commit v5 on v4

--- a/solution.py
+++ b/solution.py
@@ -34,9 +34,9 @@
     return terms if sums is None else [s + t for s, t in zip(sums, terms)]
 
 
-def columns(images, variances, taps, source, across, target, count):
+def columns(fields, taps, source, across, target, count):
     span = taps.shape[1]
-    for field, maps, base in ((images, 3, 0), (variances, 6, 3)):
+    for field, maps, base in fields:
         left = field[pl.ds(source, count), 0:LANES]
         right = field[pl.ds(source, count), LANES:]
         sums = None
@@ -52,7 +52,7 @@
                 across[base + j, side, pl.ds(target, count), :] = sums[2 * j + side]
 
 
-def row_sums(across, taps, down, tiles, offsets):
+def row_sums(across, taps, down, tiles, offsets, maps=9):
     tile = 8
     uses = {}
     for t in range(tiles):
@@ -73,7 +73,7 @@
                 down[j, side, tile * t : tile * (t + 1), :] = sums[side][t]
         return carry
 
-    lax.fori_loop(0, 9, one_map, 0, unroll=3)
+    lax.fori_loop(0, maps, one_map, 0, unroll=3)
 
 
 def combine(down, start, count, coefs, row, height, width, store):
@@ -110,6 +110,59 @@
     return jnp.broadcast_to(value, table.shape[:-1] + (LANES,))
 
 
+def two_parts(x):
+    high = x.astype(jnp.bfloat16)
+    return high, (x - high.astype(jnp.float32)).astype(jnp.bfloat16)
+
+
+def product(left, right):
+    count = left.shape[0]
+    left_high, left_low = two_parts(left)
+    right_high, right_low = right
+    both = jnp.dot(
+        jnp.concatenate([left_high, left_low]), right_high, preferred_element_type=jnp.float32
+    )
+    cross = jnp.dot(left_high, right_low, preferred_element_type=jnp.float32)
+    return both[:count] + (both[count:] + cross)
+
+
+def band(taps, j, kind, count, sign):
+    span = taps.shape[1]
+    half = span // 2
+    lane = lax.broadcasted_iota(jnp.int32, (1, LANES), 1)
+    line = jnp.zeros((1, LANES), jnp.float32)
+    for a in range(span):
+        line = jnp.where(lane == sign * (a - half) % LANES, taps[j, a, pl.ds(kind, 1), :], line)
+    line = jnp.broadcast_to(line, (count, LANES))
+    return pltpu.roll(line, 0, 1, stride=1, stride_axis=0)
+
+
+def variance_maps(variances, taps, down):
+    rows = variances.shape[1]
+    half = taps.shape[1] // 2
+    row = lax.broadcasted_iota(jnp.int32, (rows, LANES), 0)
+    lane = lax.broadcasted_iota(jnp.int32, (rows, LANES), 1)
+    near = jnp.logical_and(jnp.abs(lane - row) <= half, lane < rows)
+    row_bands = jnp.concatenate(
+        [jnp.where(near, band(taps, 3 + p, 0, rows, 1), 0.0)[:, :rows] for p in range(6)]
+    )
+    sums = product(row_bands, two_parts(variances[0]))
+    apart = lax.broadcasted_iota(jnp.int32, (LANES, LANES), 1) - lax.broadcasted_iota(
+        jnp.int32, (LANES, LANES), 0
+    )
+    for p in range(6):
+        ring = band(taps, 3 + p, 1, LANES, -1)
+        inner = jnp.where(jnp.abs(apart) <= half, ring, 0.0)
+        after = jnp.where(apart < -half, ring, 0.0)
+        before = jnp.where(apart > half, ring, 0.0)
+        column_band = jnp.concatenate(
+            [jnp.concatenate([inner, after], axis=1), jnp.concatenate([before, inner], axis=1)]
+        )
+        result = product(sums[p * rows : (p + 1) * rows], two_parts(column_band))
+        for side in range(2):
+            down[3 + p, side] = result[:, side * LANES : (side + 1) * LANES]
+
+
 def strip_is_even():
     return lax.rem(lax.axis_index("strip"), 2) == 0
 
@@ -146,7 +199,7 @@
     half = span // 2
     strip_row = lax.axis_index("strip") * rows
     height = rows * lax.axis_size("strip")
-    zero = jnp.zeros((9, 2, EDGE, LANES), jnp.float32)
+    zero = jnp.zeros((3, 2, EDGE, LANES), jnp.float32)
     across[:, :, 0:EDGE] = zero
     across[:, :, rows + EDGE :] = zero
 
@@ -162,11 +215,12 @@
 
     def inner(step, carry):
         start = pl.multiple_of(step * chunk, chunk)
-        columns(images.at[0], variances.at[0], taps, start, across, start + EDGE, chunk)
+        columns(((images.at[0], 3, 0),), taps, start, across, start + EDGE, chunk)
         return carry
 
     lax.fori_loop(0, rows // chunk, inner, 0)
-    row_sums(across, taps, down, rows // 8, [(a, EDGE - half + a) for a in range(span)])
+    row_sums(across, taps, down, rows // 8, [(a, EDGE - half + a) for a in range(span)], maps=3)
+    variance_maps(variances, taps, down)
 
     block = 32
     for start in range(0, rows, block):
@@ -187,7 +241,7 @@
     zero = jnp.zeros((9, 2, EDGE, LANES), jnp.float32)
     padded[:, :, 0:EDGE] = zero
     padded[:, :, 2 * EDGE :] = zero
-    columns(halo.at[0], halo.at[1], taps, 0, padded, EDGE, EDGE)
+    columns(((halo.at[0], 3, 0), (halo.at[1], 6, 3)), taps, 0, padded, EDGE, EDGE)
 
     @pl.when(after)
     def _():
@@ -309,7 +363,7 @@
         out_specs=[VMEM] * 3,
         out_shape=[f32(4, rows, LANES), f32(9, *kernels.shape[1:3], LANES), f32(18, LANES)],
         scratch_shapes=[
-            pltpu.VMEM((9, 2, rows + 2 * EDGE, LANES), jnp.float32),
+            pltpu.VMEM((3, 2, rows + 2 * EDGE, LANES), jnp.float32),
             pltpu.VMEM((9, 2, rows, LANES), jnp.float32),
         ],
         compiler_params=PARAMS,

time: 42.1 us -> 41.7 us (level)
  Pallas kernels: 4.97 us -> 4.5 us
    pallas_call x1, Pallas kernels: 2.29 us -> 1.82 us  [strip_parts(): pl.pallas_call(strip_kernel, in_specs=[SMEM] + [VMEM] * 6, out_specs=[VME...]
  transfers between devices with their start and end apart: 2 -> 2, of which waited for: 0 -> 1; matrix products, arithmetic and copies ran while one was open for 0% -> 0% of each run, Pallas kernels for 7% -> 6%
where the time goes in v5:
time: 41.7 us; the launch traced here: 41.5 us
  blocking collectives  29.9 us (72%)
  starting transfers between devices  5.55 us (13%)
  Pallas kernels  4.5 us (11%)
  between operations  1.38 us (3%)
    all_to_all x1, blocking collectives, shards(): lax.all_to_all(sent.reshape(rows, 4, LANES), 'visit', split_axis=0, conca...  29.9 us
    ppermute x2, starting transfers between devices, swap(): return lax.ppermute(edge, 'strip', pairs + [(b, a) for a, b in pairs])  5.55 us
    pallas_call x1, Pallas kernels, strip_parts(): pl.pallas_call(strip_kernel, in_specs=[SMEM] + [VMEM] * 6, out_specs=[VME...  1.82 us
    pallas_call x1, Pallas kernels, loaded(): pl.pallas_call(load_kernel, in_specs=[HBM] * 5, out_specs=[VMEM] * 5, out...  1.03 us
  transfers between devices with their start and end apart: 2, of which 1 were waited for; matrix products, arithmetic and copies ran while one was open for 0% of the time, Pallas kernels for 6%

profile of v5, /device:TPU:7, one launch (start us, length us, event | category | flops | bytes accessed | tf_op | source)
XLA Modules:
  0.0 41.5 jit_solution(5080485024215340409)
XLA Ops:
  0.6 0.0 copy-start
  0.6 0.0 copy-start.1
  0.7 0.0 copy-start.2
  0.7 1.0 %shard_map.86 = (f32[3,21,2,64]{3,2,1,0:T(2,128)S(1)}, f32[3,64]{1,0:T(4,128)S(1)}, f32[5,3,64]{2,1,0:T(4,128)S(1)}, f32[2,16,256]{2,1,0:T(8,128)S(1)}, f32[2,16,256]{2,1,0:T(8,128)S(1)}) custom-call(f32[3,21,2,64]{3,2,1,0:T(2,128)} %bitcast.7, f32[3,64]{1,0:T(4,128)} %bitcast.9, f32[5,3,64]{2,1,0:T(4,128)} %bitcast.8, f32[1,64,256]{2,1,0:T(8,128)} %images.3, ...), custom_call_target="tpu_custom_call" | custom-call | tf_op jit(solution)/shard_map/pallas_call | solution.py:337
  1.7 3.2 %collective-permute-start = (f32[2,16,256]{2,1,0:T(8,128)S(1)}, f32[2,16,256]{2,1,0:T(8,128)S(1)}, u32[]{:S(2)}, u32[]{:S(2)}) collective-permute-start(f32[2,16,256]{2,1,0:T(8,128)S(1)} %get-tuple-element.14), channel_id=1, source_target_pairs={{0,1},{2,3},{4,5},{6,7},{1,0},{3,2},{5,4},{7,6},{8,9},{10,11},{12,... | collective-permute-start | bytes 98312 | tf_op jit(solution)/shard_map/ppermute | solution.py:427
  4.9 2.3 %collective-permute-start.1 = (f32[2,16,256]{2,1,0:T(8,128)S(1)}, f32[2,16,256]{2,1,0:T(8,128)S(1)}, u32[]{:S(2)}, u32[]{:S(2)}) collective-permute-start(f32[2,16,256]{2,1,0:T(8,128)S(1)} %get-tuple-element.17), channel_id=1, source_target_pairs={{1,2},{3,4},{5,6},{2,1},{4,3},{6,5},{9,10},{11,12},{13,14},{10,9},... | collective-permute-start | bytes 98312 | tf_op jit(solution)/shard_map/ppermute | solution.py:427
  7.9 0.0 copy-done
  7.9 0.0 copy-done.1
  7.9 0.0 copy-done.2
  7.9 1.8 %shard_map.87 = (f32[4,64,128]{2,1,0:T(8,128)S(1)}, f32[9,21,2,128]{3,2,1,0:T(2,128)S(1)}, f32[18,128]{1,0:T(8,128)S(1)}) custom-call(s32[1]{0:T(128)S(6)} %copy.9.ids, f32[3,21,2,64]{3,2,1,0:T(2,128)S(1)} %get-tuple-element.10.tap_table, f32[3,64]{1,0:T(4,128)S(1)} %get-tuple-element.11.amplitude_table, f32[5,3,64]{2,1,0:T(4,128)S(1)} %get-tuple-element.12.shape_table, ...), custom_call_target="tpu_custom_call" | custom-call | flops 20000000 | bytes 1048576 | tf_op jit(solution)/shard_map/pallas_call | solution.py:360
  9.8 0.0 collective-permute-done.halo
  9.8 0.5 %shard_map.88.first = f32[4,16,128]{2,1,0:T(8,128)S(1)} custom-call(f32[2,16,256]{2,1,0:T(8,128)S(1)} %collective-permute-done.halo, f32[9,21,2,128]{3,2,1,0:T(2,128)S(1)} %get-tuple-element.15.taps, f32[18,128]{1,0:T(8,128)S(1)} %get-tuple-element.16.coefs), custom_call_target="tpu_custom_call" | custom-call | flops 4000000 | bytes 1048576 | tf_op jit(solution)/shard_map/pallas_call | solution.py:381
  10.3 0.2 collective-permute-done.1.halo
  10.5 0.5 %shard_map.89 = f32[256,128]{1,0:T(8,128)S(1)} custom-call(f32[4,64,128]{2,1,0:T(8,128)S(1)} %get-tuple-element.13.own, f32[4,16,128]{2,1,0:T(8,128)S(1)} %shard_map.88.first, f32[2,16,256]{2,1,0:T(8,128)S(1)} %collective-permute-done.1.halo, f32[9,21,2,128]{3,2,1,0:T(2,128)S(1)} %get-tuple-element.15.taps, f32[18,128]{1,0:T(8,128)S(1)} %get-tuple-element.16.coefs), custom_call_target="tpu_custom_call" | custom-call | tf_op jit(solution)/shard_map/pallas_call | solution.py:394
  11.0 29.9 %all_to_all.5 = f32[64,4,128]{2,1,0:T(4,128)S(1)} all-to-all(f32[64,4,128]{2,1,0:T(4,128)S(1)} %bitcast.6), channel_id=1, replica_groups=mesh['visit'=64,'strip'=8] {'visit'}, dimensions={0} | all-to-all | bytes 262144 | tf_op jit(solution)/shard_map/all_to_all | solution.py:440
  40.9 0.7 %shard_map.90 = (f32[1,256]{1,0:T(1,128)}, f32[1,256]{1,0:T(1,128)}) custom-call(f32[256,128]{1,0:T(8,128)S(1)} %bitcast.5), custom_call_target="tpu_custom_call" | custom-call | tf_op jit(solution)/shard_map/pallas_call | solution.py:405
Async XLA Ops:
  0.6 7.3 %copy-start = (f32[1,64,256]{2,1,0:T(8,128)S(1)}, f32[1,64,256]{2,1,0:T(8,128)}, u32[]{:S(2)}) copy-start(f32[1,64,256]{2,1,0:T(8,128)} %images.3) | copy-start | bytes 196612
  0.6 7.3 %copy-start.1 = (f32[1,64,256]{2,1,0:T(8,128)S(1)}, f32[1,64,256]{2,1,0:T(8,128)}, u32[]{:S(2)}) copy-start(f32[1,64,256]{2,1,0:T(8,128)} %variances.3) | copy-start | bytes 196612
  0.7 7.3 %copy-start.2 = (s32[1,64,256]{2,1,0:T(8,128)S(1)}, s32[1,64,256]{2,1,0:T(8,128)}, u32[]{:S(2)}) copy-start(s32[1,64,256]{2,1,0:T(8,128)} %masks.1) | copy-start | bytes 196612
  1.7 8.1 %collective-permute-start = (f32[2,16,256]{2,1,0:T(8,128)S(1)}, f32[2,16,256]{2,1,0:T(8,128)S(1)}, u32[]{:S(2)}, u32[]{:S(2)}) collective-permute-start(f32[2,16,256]{2,1,0:T(8,128)S(1)} %get-tuple-element.14), channel_id=1, source_target_pairs={{0,1},{2,3},{4,5},{6,7},{1,0},{3,2},{5,4},{7,6},{8,9},{10,11},{12,... | collective-permute-start | bytes 98312 | tf_op jit(solution)/shard_map/ppermute | solution.py:427
  4.9 5.6 %collective-permute-start.1 = (f32[2,16,256]{2,1,0:T(8,128)S(1)}, f32[2,16,256]{2,1,0:T(8,128)S(1)}, u32[]{:S(2)}, u32[]{:S(2)}) collective-permute-start(f32[2,16,256]{2,1,0:T(8,128)S(1)} %get-tuple-element.17), channel_id=1, source_target_pairs={{1,2},{3,4},{5,6},{2,1},{4,3},{6,5},{9,10},{11,12},{13,14},{10,9},... | collective-permute-start | bytes 98312 | tf_op jit(solution)/shard_map/ppermute | solution.py:427

commit v6 on v5

--- a/solution.py
+++ b/solution.py
@@ -167,38 +167,35 @@
     return lax.rem(lax.axis_index("strip"), 2) == 0
 
 
-def load_kernel(
-    kernels, amplitudes, shapes, images, variances,
-    tap_table, amplitude_table, shape_table, sent_first, sent_second, sems,
-):
+def load_kernel(images, variances, image_rows, variance_rows, sent_first, sent_second, sems):
     rows = images.shape[1]
+    copies = [
+        pltpu.make_async_copy(images, image_rows, sems.at[0]),
+        pltpu.make_async_copy(variances, variance_rows, sems.at[1]),
+    ]
+    for copy in copies:
+        copy.start()
     place = pl.multiple_of(jnp.where(strip_is_even(), rows - EDGE, 0), EDGE)
     other = pl.multiple_of(jnp.where(strip_is_even(), 0, rows - EDGE), EDGE)
-    copies = [
-        (images.at[0, pl.ds(place, EDGE)], sent_first.at[0]),
-        (variances.at[0, pl.ds(place, EDGE)], sent_first.at[1]),
-        (images.at[0, pl.ds(other, EDGE)], sent_second.at[0]),
-        (variances.at[0, pl.ds(other, EDGE)], sent_second.at[1]),
-        (kernels, tap_table),
-        (amplitudes, amplitude_table),
-        (shapes, shape_table),
-    ]
-    copies = [pltpu.make_async_copy(a, b, sems.at[i]) for i, (a, b) in enumerate(copies)]
-    for copy in copies:
-        copy.start()
-    for copy in copies:
-        copy.wait()
+    for i, field in enumerate((image_rows, variance_rows)):
+        copies[i].wait()
+        sent_first[i] = field[0, pl.ds(place, EDGE)]
+        sent_second[i] = field[0, pl.ds(other, EDGE)]
 
 
 def strip_kernel(
-    ids, tap_table, amplitude_table, shape_table, images, variances, masks,
-    out, taps, coefs, across, down,
+    ids, tap_table, amplitudes, shapes, images, variances, masks,
+    out, taps, coefs, across, down, amplitude_table, shape_table, mask, sems,
 ):
     rows, width = images.shape[1:]
     span = taps.shape[1]
     half = span // 2
     strip_row = lax.axis_index("strip") * rows
     height = rows * lax.axis_size("strip")
+    copies = [(amplitudes, amplitude_table), (shapes, shape_table), (masks, mask)]
+    copies = [pltpu.make_async_copy(a, b, sems.at[i]) for i, (a, b) in enumerate(copies)]
+    for copy in copies:
+        copy.start()
     zero = jnp.zeros((3, 2, EDGE, LANES), jnp.float32)
     across[:, :, 0:EDGE] = zero
     across[:, :, rows + EDGE :] = zero
@@ -207,10 +204,6 @@
     taps[0:3] = of_visit(visit, tap_table[...])
     for p, (i, j) in enumerate(zip(pair_first, pair_second)):
         taps[3 + p] = taps[i] * taps[j]
-    for t in range(5):
-        coefs[3 * t : 3 * t + 3] = of_visit(visit, shape_table[t])
-    coefs[15:18] = of_visit(visit, amplitude_table[...])
-
     chunk = 32
 
     def inner(step, carry):
@@ -220,6 +213,11 @@
 
     lax.fori_loop(0, rows // chunk, inner, 0)
     row_sums(across, taps, down, rows // 8, [(a, EDGE - half + a) for a in range(span)], maps=3)
+    for copy in copies:
+        copy.wait()
+    for t in range(5):
+        coefs[3 * t : 3 * t + 3] = of_visit(visit, shape_table[t])
+    coefs[15:18] = of_visit(visit, amplitude_table[...])
     variance_maps(variances, taps, down)
 
     block = 32
@@ -227,8 +225,8 @@
         row = lax.broadcasted_iota(jnp.int32, (block, LANES), 0) + (start + strip_row)
 
         def store(side, matched, spread):
-            mask = masks[0, pl.ds(start, block), side * LANES : (side + 1) * LANES]
-            valid = jnp.bitwise_and(mask, 7) == 0
+            bits = mask[0, pl.ds(start, block), side * LANES : (side + 1) * LANES]
+            valid = jnp.bitwise_and(bits, 7) == 0
             out[side, pl.ds(start, block), :] = matched
             out[2 + side, pl.ds(start, block), :] = jnp.where(valid, spread, jnp.inf)
 
@@ -332,43 +330,44 @@
     return pl.CostEstimate(flops=flops, bytes_accessed=1 << 20, transcendentals=0)
 
 
-def loaded(kernels, amplitudes, shapes, images, variances):
+def loaded(images, variances):
     width = images.shape[2]
     return pl.pallas_call(
         load_kernel,
-        in_specs=[HBM] * 5,
-        out_specs=[VMEM] * 5,
-        out_shape=[
-            f32(*kernels.shape),
-            f32(*amplitudes.shape),
-            f32(*shapes.shape),
-            f32(2, EDGE, width),
-            f32(2, EDGE, width),
-        ],
-        scratch_shapes=[pltpu.SemaphoreType.DMA((7,))],
+        in_specs=[HBM] * 2,
+        out_specs=[VMEM] * 4,
+        out_shape=[f32(*images.shape)] * 2 + [f32(2, EDGE, width)] * 2,
+        scratch_shapes=[pltpu.SemaphoreType.DMA((2,))],
         compiler_params=PARAMS,
-    )(
-        *(
-            pltpu.with_memory_space_constraint(x, pltpu.HBM)
-            for x in (kernels, amplitudes, shapes, images, variances)
-        )
-    )
+    )(*(pltpu.with_memory_space_constraint(x, pltpu.HBM) for x in (images, variances)))
 
 
 def strip_parts(ids, kernels, amplitudes, shapes, images, variances, masks):
     rows = images.shape[1]
     return pl.pallas_call(
         strip_kernel,
-        in_specs=[SMEM] + [VMEM] * 6,
+        in_specs=[SMEM, VMEM] + [HBM] * 2 + [VMEM] * 2 + [HBM],
         out_specs=[VMEM] * 3,
         out_shape=[f32(4, rows, LANES), f32(9, *kernels.shape[1:3], LANES), f32(18, LANES)],
         scratch_shapes=[
             pltpu.VMEM((3, 2, rows + 2 * EDGE, LANES), jnp.float32),
             pltpu.VMEM((9, 2, rows, LANES), jnp.float32),
+            pltpu.VMEM(amplitudes.shape, jnp.float32),
+            pltpu.VMEM(shapes.shape, jnp.float32),
+            pltpu.VMEM(masks.shape, jnp.int32),
+            pltpu.SemaphoreType.DMA((3,)),
         ],
         compiler_params=PARAMS,
         cost_estimate=cost(20_000_000),
-    )(ids, kernels, amplitudes, shapes, images, variances, masks)
+    )(
+        ids,
+        kernels,
+        pltpu.with_memory_space_constraint(amplitudes, pltpu.HBM),
+        pltpu.with_memory_space_constraint(shapes, pltpu.HBM),
+        images,
+        variances,
+        pltpu.with_memory_space_constraint(masks, pltpu.HBM),
+    )
 
 
 HALO_SCRATCH = [
@@ -414,12 +413,11 @@
 def before_exchange(images, variances, masks, visit_ids, kernels, amplitudes, shapes):
     strips = lax.axis_size("strip")
     rows = images.shape[1]
-    *tables, sent_first, sent_second = loaded(
+    image_rows, variance_rows, sent_first, sent_second = loaded(images, variances)
+    tables = (
         jnp.transpose(kernels, (1, 3, 2, 0)),
         jnp.transpose(amplitudes, (1, 0)),
         jnp.transpose(shapes, (2, 1, 0)),
-        images,
-        variances,
     )
 
     def swap(edge, start):
@@ -428,7 +426,7 @@
 
     halo_first = swap(sent_first, 0)
     halo_second = swap(sent_second, 1)
-    own, taps, coefs = strip_parts(visit_ids, *tables, images, variances, masks)
+    own, taps, coefs = strip_parts(visit_ids, *tables, image_rows, variance_rows, masks)
     first = first_part(rows, halo_first, taps, coefs)
     return weighted(own, first, halo_second, taps, coefs)
 

time: 41.7 us -> 41.6 us (level)
  no operation moved by 1% of the time
where the time goes in v6:
time: 41.6 us; the launch traced here: 41.4 us
  blocking collectives  29.9 us (72%)
  starting transfers between devices  5.55 us (13%)
  Pallas kernels  4.46 us (11%)
  between operations  1.34 us (3%)
    all_to_all x1, blocking collectives, shards(): lax.all_to_all(sent.reshape(rows, 4, LANES), 'visit', split_axis=0, conca...  29.9 us
    ppermute x2, starting transfers between devices, swap(): return lax.ppermute(edge, 'strip', pairs + [(b, a) for a, b in pairs])  5.55 us
    pallas_call x1, Pallas kernels, strip_parts(): pl.pallas_call(strip_kernel, in_specs=[SMEM, VMEM] + [HBM] * 2 + [VMEM] *...  1.9 us
    pallas_call x1, Pallas kernels, loaded(): pl.pallas_call(load_kernel, in_specs=[HBM] * 2, out_specs=[VMEM] * 4, out...  0.91 us
  transfers between devices with their start and end apart: 2, of which 1 were waited for; matrix products, arithmetic and copies ran while one was open for 0% of the time, Pallas kernels for 6%

profile of v6, /device:TPU:7, one launch (start us, length us, event | category | flops | bytes accessed | tf_op | source)
XLA Modules:
  0.0 41.4 jit_solution(10395832815476099496)
XLA Ops:
  0.6 0.0 copy-start
  0.6 0.9 %shard_map.86 = (f32[1,64,256]{2,1,0:T(8,128)S(1)}, f32[1,64,256]{2,1,0:T(8,128)S(1)}, f32[2,16,256]{2,1,0:T(8,128)S(1)}, f32[2,16,256]{2,1,0:T(8,128)S(1)}) custom-call(f32[1,64,256]{2,1,0:T(8,128)} %images.1, f32[1,64,256]{2,1,0:T(8,128)} %variances.1), custom_call_target="tpu_custom_call" | custom-call | tf_op jit(solution)/shard_map/pallas_call | solution.py:335
  1.6 3.2 %collective-permute-start = (f32[2,16,256]{2,1,0:T(8,128)S(1)}, f32[2,16,256]{2,1,0:T(8,128)S(1)}, u32[]{:S(2)}, u32[]{:S(2)}) collective-permute-start(f32[2,16,256]{2,1,0:T(8,128)S(1)} %get-tuple-element.12), channel_id=1, source_target_pairs={{0,1},{2,3},{4,5},{6,7},{1,0},{3,2},{5,4},{7,6},{8,9},{10,11},{12,... | collective-permute-start | bytes 98312 | tf_op jit(solution)/shard_map/ppermute | solution.py:425
  4.8 2.3 %collective-permute-start.1 = (f32[2,16,256]{2,1,0:T(8,128)S(1)}, f32[2,16,256]{2,1,0:T(8,128)S(1)}, u32[]{:S(2)}, u32[]{:S(2)}) collective-permute-start(f32[2,16,256]{2,1,0:T(8,128)S(1)} %get-tuple-element.15), channel_id=1, source_target_pairs={{1,2},{3,4},{5,6},{2,1},{4,3},{6,5},{9,10},{11,12},{13,14},{10,9},... | collective-permute-start | bytes 98312 | tf_op jit(solution)/shard_map/ppermute | solution.py:425
  7.8 0.0 copy-done
  7.8 1.9 %shard_map.87 = (f32[4,64,128]{2,1,0:T(8,128)S(1)}, f32[9,21,2,128]{3,2,1,0:T(2,128)S(1)}, f32[18,128]{1,0:T(8,128)S(1)}) custom-call(s32[1]{0:T(128)S(6)} %copy.9.ids, f32[3,21,2,64]{3,2,1,0:T(2,128)S(1)} %bitcast.7, f32[3,64]{1,0:T(4,128)} %bitcast.9, f32[5,3,64]{2,1,0:T(4,128)} %bitcast.8, f32[1,64,256]{2,1,0:T(8,128)S(1)} %get-tuple-element.9.images, ...), custom_call_target="tpu_custom_call" | custom-call | flops 20000000 | bytes 1048576 | tf_op jit(solution)/shard_map/pallas_call | solution.py:347
  9.7 0.0 collective-permute-done.halo
  9.7 0.5 %shard_map.88.first = f32[4,16,128]{2,1,0:T(8,128)S(1)} custom-call(f32[2,16,256]{2,1,0:T(8,128)S(1)} %collective-permute-done.halo, f32[9,21,2,128]{3,2,1,0:T(2,128)S(1)} %get-tuple-element.13.taps, f32[18,128]{1,0:T(8,128)S(1)} %get-tuple-element.14.coefs), custom_call_target="tpu_custom_call" | custom-call | flops 4000000 | bytes 1048576 | tf_op jit(solution)/shard_map/pallas_call | solution.py:380
  10.2 0.1 collective-permute-done.1.halo
  10.3 0.5 %shard_map.89 = f32[256,128]{1,0:T(8,128)S(1)} custom-call(f32[4,64,128]{2,1,0:T(8,128)S(1)} %get-tuple-element.11.own, f32[4,16,128]{2,1,0:T(8,128)S(1)} %shard_map.88.first, f32[2,16,256]{2,1,0:T(8,128)S(1)} %collective-permute-done.1.halo, f32[9,21,2,128]{3,2,1,0:T(2,128)S(1)} %get-tuple-element.13.taps, f32[18,128]{1,0:T(8,128)S(1)} %get-tuple-element.14.coefs), custom_call_target="tpu_custom_call" | custom-call | tf_op jit(solution)/shard_map/pallas_call | solution.py:393
  10.8 29.9 %all_to_all.5 = f32[64,4,128]{2,1,0:T(4,128)S(1)} all-to-all(f32[64,4,128]{2,1,0:T(4,128)S(1)} %bitcast.6), channel_id=1, replica_groups=mesh['visit'=64,'strip'=8] {'visit'}, dimensions={0} | all-to-all | bytes 262144 | tf_op jit(solution)/shard_map/all_to_all | solution.py:438
  40.8 0.7 %shard_map.90 = (f32[1,256]{1,0:T(1,128)}, f32[1,256]{1,0:T(1,128)}) custom-call(f32[256,128]{1,0:T(8,128)S(1)} %bitcast.5), custom_call_target="tpu_custom_call" | custom-call | tf_op jit(solution)/shard_map/pallas_call | solution.py:404
Async XLA Ops:
  0.6 7.1 %copy-start = (f32[64,3,2,21]{0,2,3,1:T(2,128)S(1)}, f32[64,3,2,21]{0,2,3,1:T(2,128)}, u32[]{:S(2)}) copy-start(f32[64,3,2,21]{0,2,3,1:T(2,128)} %param.11) | copy-start | bytes 96772
  1.6 8.1 %collective-permute-start = (f32[2,16,256]{2,1,0:T(8,128)S(1)}, f32[2,16,256]{2,1,0:T(8,128)S(1)}, u32[]{:S(2)}, u32[]{:S(2)}) collective-permute-start(f32[2,16,256]{2,1,0:T(8,128)S(1)} %get-tuple-element.12), channel_id=1, source_target_pairs={{0,1},{2,3},{4,5},{6,7},{1,0},{3,2},{5,4},{7,6},{8,9},{10,11},{12,... | collective-permute-start | bytes 98312 | tf_op jit(solution)/shard_map/ppermute | solution.py:425
  4.8 5.6 %collective-permute-start.1 = (f32[2,16,256]{2,1,0:T(8,128)S(1)}, f32[2,16,256]{2,1,0:T(8,128)S(1)}, u32[]{:S(2)}, u32[]{:S(2)}) collective-permute-start(f32[2,16,256]{2,1,0:T(8,128)S(1)} %get-tuple-element.15), channel_id=1, source_target_pairs={{1,2},{3,4},{5,6},{2,1},{4,3},{6,5},{9,10},{11,12},{13,14},{10,9},... | collective-permute-start | bytes 98312 | tf_op jit(solution)/shard_map/ppermute | solution.py:425
